TPU v7x, 32 devices: a whole 2x2x4 slice. The times are simulated.
32 devices in a mesh: dp: 8 (over z, y), tensor: 4 (over x, core).
Axes of the slice: x: 2, y: 2, z: 4, core: 2. Of those that a mesh axis runs over, the one named last changes fastest.
Arguments:
- tokens: bfloat16 [4096, 1024], P(('dp', 'tensor')), may hold values from -6 to 6
- cotangent: bfloat16 [4096, 1024], P(('dp', 'tensor')), may hold values from -6 to 6
- seg_lengths: int32 [8, 4], P('dp'), may hold values from 0 to 512, as said below
- vectors: float32 [6, 1024], P(None, 'dp'), may hold values from -2 to 2
- w_qkv: bfloat16 [1024, 3, 1024], P('dp', None, 'tensor'), may hold values from -0.1875 to 0.1875
- qv_bias: float32 [2, 16, 64], P(None, 'tensor', 'dp'), may hold values from -3 to 3
- w_out: bfloat16 [1024, 1024], P('tensor', 'dp'), may hold values from -0.5 to 0.5
- w_up: bfloat16 [1024, 4096], P('dp', 'tensor'), may hold values from -0.1875 to 0.1875
- up_bias: float32 [16, 256], P('tensor', 'dp'), may hold values from -3 to 3
- w_down: bfloat16 [4096, 1024], P('tensor', 'dp'), may hold values from -0.125 to 0.125
Outputs:
- output: bfloat16 [4096, 1024], P(('dp', 'tensor'))
- grad_tokens: bfloat16 [4096, 1024], P(('dp', 'tensor'))
- grad_vectors: float32 [6, 1024], P(None, 'dp')
- grad_qkv: float32 [1024, 3, 1024], P('dp', None, 'tensor')
- grad_qv_bias: float32 [2, 16, 64], P(None, 'tensor', 'dp')
- grad_out: float32 [1024, 1024], P('tensor', 'dp')
- grad_up: float32 [1024, 4096], P('dp', 'tensor')
- grad_up_bias: float32 [16, 256], P('tensor', 'dp')
- grad_down: float32 [4096, 1024], P('tensor', 'dp')
Inputs may be any that keep to these rules, and one draw needn't show every extreme that they name: `seg_lengths`: each row gives, in order, the lengths of the 4 documents that fill the 512 positions of one group; a row sums to 512; a zero is an empty document; the first document of every group is longer than 384.
All inputs are finite; a program needn't handle non-finite values.
Results may differ from a plain program's by a relative error of at most 0.03.
Values may be sent and summed in bfloat16 or wider, within the bound.
A program may use at most 64 MiB of HBM per device.

v0:
```python
import jax
import jax.numpy as jnp
from jax import lax
from jax.sharding import PartitionSpec as P

epsilon = 1e-05
masked_score = -1e30


def layer_norm(values, gain_vec, shift_vec):
    center = values - jnp.mean(values, axis=-1, keepdims=True)
    spread = jnp.mean(center * center, axis=-1, keepdims=True)
    return center * lax.rsqrt(spread + epsilon) * gain_vec + shift_vec


def gelu_tanh(values):
    return jax.nn.gelu(values, approximate=True)


def doc_number(positions, lengths):
    doc_ends = jnp.cumsum(lengths)
    return jnp.sum((positions[:, None] >= doc_ends[None, :]).astype(jnp.int32), axis=1)


def block_scores(query_block, key_heads, first_row, slopes, lengths):
    block_size = query_block.shape[0]
    group_size = key_heads.shape[0]
    score_scale = query_block.shape[-1] ** (-0.5)
    scores = (
        jnp.einsum("qhd,khd->hqk", query_block, key_heads, preferred_element_type=jnp.float32)
        * score_scale
    )
    query_pos = first_row + jnp.arange(block_size, dtype=jnp.int32)
    key_pos = jnp.arange(group_size, dtype=jnp.int32)
    offset = (query_pos[:, None] - key_pos[None, :]).astype(jnp.float32)
    scores = scores - slopes[:, None, None] * offset[None]
    same_doc = doc_number(query_pos, lengths)[:, None] == doc_number(key_pos, lengths)[None, :]
    allowed = same_doc & (key_pos[None, :] <= query_pos[:, None])
    return jnp.where(allowed[None], scores, masked_score)


def on_device(
    tokens, cotangent, seg_lengths, vectors, w_qkv, qv_bias, w_out, w_up, up_bias, w_down
):
    model_width = tokens.shape[1]
    tensor_count = lax.axis_size("tensor")
    lengths = seg_lengths[0]
    gathered = (
        lax.all_gather(w_qkv, "dp", axis=0, tiled=True),
        lax.all_gather(qv_bias.astype(jnp.bfloat16), "dp", axis=2, tiled=True).astype(
            qv_bias.dtype
        ),
        lax.all_gather(w_out, "dp", axis=1, tiled=True),
        lax.all_gather(w_up, "dp", axis=0, tiled=True),
        lax.all_gather(up_bias.astype(jnp.bfloat16), "dp", axis=1, tiled=True).astype(
            up_bias.dtype
        ),
        lax.all_gather(w_down, "dp", axis=1, tiled=True),
        lax.all_gather(vectors.astype(jnp.bfloat16), "dp", axis=1, tiled=True).astype(
            vectors.dtype
        ),
    )
    qkv_full, bias_full, out_full, up_full, upbias_full, down_full, vec_full = gathered
    local_width = qkv_full.shape[2]
    heads_local = bias_full.shape[1]
    head_size = bias_full.shape[2]
    hidden_local = up_full.shape[1]
    head_ids = lax.axis_index("tensor") * heads_local + jnp.arange(heads_local, dtype=jnp.int32)
    slopes = jnp.exp2(-8.0 * (head_ids + 1).astype(jnp.float32) / (heads_local * tensor_count))
    inputs = tokens.astype(jnp.float32)
    normed_one = layer_norm(inputs, vec_full[0], vec_full[1]).astype(jnp.bfloat16)
    group_one = lax.all_gather(normed_one, "tensor", axis=0, tiled=True)
    group_size = group_one.shape[0]
    projected = jnp.dot(
        group_one,
        qkv_full.reshape(model_width, 3 * local_width),
        preferred_element_type=jnp.float32,
    )
    projected = projected.reshape(group_size, 3, local_width)
    head_shape = (group_size, heads_local, head_size)
    query_heads = (
        (projected[:, 0] + bias_full[0].reshape(local_width))
        .astype(jnp.bfloat16)
        .reshape(head_shape)
    )
    key_heads = projected[:, 1].astype(jnp.bfloat16).reshape(head_shape)
    value_heads = (
        (projected[:, 2] + bias_full[1].reshape(local_width))
        .astype(jnp.bfloat16)
        .reshape(head_shape)
    )
    block_index = 0
    first_row = block_index * group_size
    scores = block_scores(query_heads, key_heads, first_row, slopes, lengths)
    row_max = jnp.max(scores, axis=-1, keepdims=True)
    exponent = jnp.exp(scores - row_max)
    row_sum = jnp.sum(exponent, axis=-1, keepdims=True)
    weights = (exponent / row_sum).astype(jnp.bfloat16)
    out_blocks = jnp.einsum(
        "hqk,khd->qhd", weights, value_heads, preferred_element_type=jnp.float32
    )
    lse_blocks = (row_max + jnp.log(row_sum))[..., 0]
    attended = out_blocks.reshape(group_size, local_width).astype(jnp.bfloat16)
    branch_attn = lax.psum_scatter(
        jnp.dot(attended, out_full, preferred_element_type=jnp.float32).astype(jnp.bfloat16),
        "tensor",
        scatter_dimension=0,
        tiled=True,
    ).astype(jnp.float32)
    middle = inputs + branch_attn + vec_full[2]
    normed_two = layer_norm(middle, vec_full[3], vec_full[4]).astype(jnp.bfloat16)
    group_two = lax.all_gather(normed_two, "tensor", axis=0, tiled=True)
    pre_act = jnp.dot(group_two, up_full, preferred_element_type=jnp.float32) + upbias_full.reshape(
        hidden_local
    )
    activated = gelu_tanh(pre_act).astype(jnp.bfloat16)
    branch_mlp = lax.psum_scatter(
        jnp.dot(activated, down_full, preferred_element_type=jnp.float32).astype(jnp.bfloat16),
        "tensor",
        scatter_dimension=0,
        tiled=True,
    ).astype(jnp.float32)
    output = (middle + branch_mlp + vec_full[5]).astype(jnp.bfloat16)
    qkv_back, out_back, up_back, down_back = (
        lax.all_gather(w_qkv, "dp", axis=0, tiled=True),
        lax.all_gather(w_out, "dp", axis=1, tiled=True),
        lax.all_gather(w_up, "dp", axis=0, tiled=True),
        lax.all_gather(w_down, "dp", axis=1, tiled=True),
    )
    grad_output = cotangent.astype(jnp.float32)
    grad_mlp = grad_output.astype(jnp.bfloat16)
    shard_rows = lax.all_gather(grad_mlp, "tensor", axis=0, tiled=True)
    used_rows = activated
    grad_weight = lax.dot_general(
        used_rows, shard_rows, (((0,), (0,)), ((), ())), preferred_element_type=jnp.float32
    )
    partial_value = lax.dot_general(
        shard_rows, down_back, (((1,), (1,)), ((), ())), preferred_element_type=jnp.float32
    )
    grad_down = grad_weight
    grad_act = partial_value
    _, gelu_back = jax.vjp(gelu_tanh, pre_act)
    grad_pre = gelu_back(grad_act)[0].astype(jnp.bfloat16)
    grad_upbias = jnp.sum(grad_pre.astype(jnp.float32), axis=0).reshape(upbias_full.shape)
    grad_up = lax.dot_general(
        group_two, grad_pre, (((0,), (0,)), ((), ())), preferred_element_type=jnp.float32
    )
    used_rows = grad_pre
    grad_normed_two = lax.psum_scatter(
        lax.dot_general(
            used_rows, up_back, (((1,), (1,)), ((), ())), preferred_element_type=jnp.float32
        ).astype(jnp.bfloat16),
        "tensor",
        scatter_dimension=0,
        tiled=True,
    ).astype(jnp.float32)
    _, norm_two_back = jax.vjp(layer_norm, middle, vec_full[3], vec_full[4])
    grad_mid_norm, grad_gain_two, grad_shift_two = norm_two_back(grad_normed_two)
    grad_middle = grad_output + grad_mid_norm
    grad_attn = grad_middle.astype(jnp.bfloat16)
    shard_rows = lax.all_gather(grad_attn, "tensor", axis=0, tiled=True)
    used_rows = attended
    grad_weight = lax.dot_general(
        used_rows, shard_rows, (((0,), (0,)), ((), ())), preferred_element_type=jnp.float32
    )
    partial_value = lax.dot_general(
        shard_rows, out_back, (((1,), (1,)), ((), ())), preferred_element_type=jnp.float32
    )
    grad_heads = partial_value.astype(jnp.bfloat16).reshape(head_shape)
    score_scale = head_size ** (-0.5)
    block_index = 0
    first_row = block_index * group_size
    scores = block_scores(query_heads, key_heads, first_row, slopes, lengths)
    probs = jnp.exp(scores - lse_blocks[:, first_row : first_row + group_size, None])
    weights = probs.astype(jnp.bfloat16)
    grad_probs = jnp.einsum(
        "qhd,khd->hqk", grad_heads, value_heads, preferred_element_type=jnp.float32
    )
    row_term = jnp.sum(probs * grad_probs, axis=-1, keepdims=True)
    grad_scores = (probs * (grad_probs - row_term)).astype(jnp.bfloat16)
    query_parts = (
        jnp.einsum("hqk,khd->qhd", grad_scores, key_heads, preferred_element_type=jnp.float32)
        * score_scale
    )
    grad_keys = (
        jnp.einsum("hqk,qhd->khd", grad_scores, query_heads, preferred_element_type=jnp.float32)
        * score_scale
    )
    grad_values = jnp.einsum(
        "hqk,qhd->khd", weights, grad_heads, preferred_element_type=jnp.float32
    )
    grad_query = query_parts.reshape(group_size, local_width).astype(jnp.bfloat16)
    grad_key = grad_keys.reshape(group_size, local_width).astype(jnp.bfloat16)
    grad_value = grad_values.reshape(group_size, local_width).astype(jnp.bfloat16)
    grad_proj = jnp.stack([grad_query, grad_key, grad_value], axis=1)
    grad_qvbias = jnp.stack(
        [
            jnp.sum(grad_query.astype(jnp.float32), axis=0),
            jnp.sum(grad_value.astype(jnp.float32), axis=0),
        ]
    ).reshape(bias_full.shape)
    grad_qkv = lax.dot_general(
        group_one, grad_proj, (((0,), (0,)), ((), ())), preferred_element_type=jnp.float32
    )
    used_rows = grad_proj
    grad_normed_one = lax.psum_scatter(
        lax.dot_general(
            used_rows, qkv_back, (((1, 2), (1, 2)), ((), ())), preferred_element_type=jnp.float32
        ).astype(jnp.bfloat16),
        "tensor",
        scatter_dimension=0,
        tiled=True,
    ).astype(jnp.float32)
    _, norm_one_back = jax.vjp(layer_norm, inputs, vec_full[0], vec_full[1])
    grad_in_norm, grad_gain_one, grad_shift_one = norm_one_back(grad_normed_one)
    grad_tokens = (grad_middle + grad_in_norm).astype(jnp.bfloat16)
    grad_vecs = jnp.stack(
        [
            grad_gain_one,
            grad_shift_one,
            jnp.sum(grad_middle, axis=0),
            grad_gain_two,
            grad_shift_two,
            jnp.sum(grad_output, axis=0),
        ]
    )
    sent_qkv, sent_qvbias, sent_out, sent_up, sent_upbias, sent_down, sent_vecs = (
        lax.psum_scatter(grad_qkv, "dp", scatter_dimension=0, tiled=True),
        lax.psum_scatter(grad_qvbias, "dp", scatter_dimension=2, tiled=True),
        lax.psum_scatter(grad_weight, "dp", scatter_dimension=1, tiled=True),
        lax.psum_scatter(grad_up, "dp", scatter_dimension=0, tiled=True),
        lax.psum_scatter(grad_upbias, "dp", scatter_dimension=1, tiled=True),
        lax.psum_scatter(grad_down, "dp", scatter_dimension=1, tiled=True),
        lax.psum_scatter(grad_vecs, "dp", scatter_dimension=1, tiled=True),
    )
    sent_vecs = lax.psum(sent_vecs, "tensor")
    return (
        output,
        grad_tokens,
        sent_vecs,
        sent_qkv,
        sent_qvbias,
        sent_out,
        sent_up,
        sent_upbias,
        sent_down,
    )


def solution(mesh):
    return jax.shard_map(
        on_device,
        mesh=mesh,
        in_specs=(
            P(("dp", "tensor"), None),
            P(("dp", "tensor"), None),
            P("dp", None),
            P(None, "dp"),
            P("dp", None, "tensor"),
            P(None, "tensor", "dp"),
            P("tensor", "dp"),
            P("dp", "tensor"),
            P("tensor", "dp"),
            P("tensor", "dp"),
        ),
        out_specs=(
            P(("dp", "tensor"), None),
            P(("dp", "tensor"), None),
            P(None, "dp"),
            P("dp", None, "tensor"),
            P(None, "tensor", "dp"),
            P("tensor", "dp"),
            P("dp", "tensor"),
            P("tensor", "dp"),
            P("tensor", "dp"),
        ),
        check_vma=False,
    )
```

profile of v0, /device:TPU:0, one launch (start us, length us, event | category | flops | bytes accessed | tf_op | source)
XLA Modules:
  0.0 850.1 jit_solution(9288453274700659598)
XLA Ops:
  8.7 27.9 %all_gather.37 = bf16[6,1024]{1,0:T(8,128)(2,1)S(1)} all-gather(bf16[6,128]{1,0:T(8,128)(2,1)S(1)} %convert_element_type.189), channel_id=1, replica_groups=mesh['dp'=8,'tensor'=4] {'dp'}, dimensions={1}, use_global_device_ids=true | all-gather | bytes 13824 | tf_op jit(solution)/shard_map/all_gather | solution.py:59
  37.6 1.2 fusion.36
  38.8 1.9 fusion.34
  41.6 30.5 %all_gather.40 = bf16[2,4,64]{1,0,2:T(2,128)(2,1)S(1)} all-gather(bf16[2,4,8]{1,0,2:T(2,128)(2,1)S(1)} %copy.64), channel_id=1, replica_groups=mesh['dp'=8,'tensor'=4] {'dp'}, dimensions={2}, use_global_device_ids=true | all-gather | bytes 1152 | tf_op jit(solution)/shard_map/all_gather | solution.py:50
  74.4 27.0 %all_gather.41 = bf16[256,1024]{1,0:T(8,128)(2,1)S(1)} all-gather(bf16[256,128]{1,0:T(8,128)(2,1)S(1)} %copy-done.13), channel_id=1, replica_groups=mesh['dp'=8,'tensor'=4] {'dp'}, dimensions={1}, use_global_device_ids=true | all-gather | bytes 589824 | tf_op jit(solution)/shard_map/all_gather | solution.py:53
  101.6 1.7 copy.63
  103.4 2.2 fusion.13
  106.9 1.5 fusion.56
  108.9 1.3 copy-done
  111.1 1.4 convolution_convert_fusion.2
  113.2 22.1 %reduce-scatter.14.cloned.1.call-done = bf16[128,1024]{1,0:T(8,128)(2,1)} async-done(((bf16[512,1024]{1,0:T(8,128)(2,1)}), bf16[128,1024]{1,0:T(8,128)(2,1)}) %reduce-scatter.14.cloned.1.call-update) | async-done | bytes 262160 | tf_op jit(solution)/shard_map/reduce_scatter | solution.py:104
  137.6 1.8 add_convert_fusion.2
  140.8 20.6 %all-gather = bf16[8,32,4]{1,2,0:T(4,128)(2,1)S(1)} all-gather(bf16[1,32,4]{1,2,0:T(4,128)(2,1)S(1)} %convert_bitcast_fusion), channel_id=1, replica_groups=mesh['dp'=8,'tensor'=4] {'dp'}, dimensions={0}, use_global_device_ids=true | all-gather | bytes 2304 | tf_op jit(solution)/shard_map/all_gather | solution.py:55
  161.5 25.3 %all-gather.15.cloned.1.call-done = bf16[1024,1024]{1,0:T(8,128)(2,1)} async-done(((bf16[128,1024]{1,0:T(8,128)(2,1)}), bf16[1024,1024]{1,0:T(8,128)(2,1)}) %all-gather.15.cloned.1.call-update) | async-done | bytes 2097168 | tf_op jit(solution)/shard_map/all_gather | solution.py:54
  186.8 17.3 %all-gather.13.cloned.1.call-done = bf16[512,1024]{1,0:T(8,128)(2,1)} async-done(((bf16[128,1024]{1,0:T(8,128)(2,1)}), bf16[512,1024]{1,0:T(8,128)(2,1)}) %all-gather.13.cloned.1.call-update) | async-done | bytes 1048592 | tf_op jit(solution)/shard_map/all_gather | solution.py:112
  204.1 4.5 fusion.57
  208.6 13.8 %all-gather.19.cloned.1.call-done = bf16[512,1024]{1,0:T(8,128)(2,1)} async-done(((bf16[128,1024]{1,0:T(8,128)(2,1)}), bf16[512,1024]{1,0:T(8,128)(2,1)}) %all-gather.19.cloned.1.call-update) | async-done | bytes 1048592 | tf_op jit(solution)/shard_map/all_gather | solution.py:132
  222.4 53.4 %all-gather.17.cloned.1.call-done = bf16[1024,1024]{1,0:T(8,128)(2,1)} async-done(((bf16[1024,128]{1,0:T(8,128)(2,1)}), bf16[1024,1024]{1,0:T(8,128)(2,1)}) %all-gather.17.cloned.1.call-update) | async-done | bytes 2097168 | tf_op jit(solution)/shard_map/all_gather | solution.py:58
  275.8 5.2 convert_reduce_fusion
  281.9 2.3 convolution_convert_fusion
  284.5 4.7 convolution_convert_fusion.1
  289.3 18.2 %reduce-scatter.18.cloned.1.call-done = bf16[128,1024]{1,0:T(8,128)(2,1)} async-done(((bf16[512,1024]{1,0:T(8,128)(2,1)}), bf16[128,1024]{1,0:T(8,128)(2,1)}) %reduce-scatter.18.cloned.1.call-update) | async-done | bytes 262160 | tf_op jit(solution)/shard_map/reduce_scatter | solution.py:149
  307.5 1.2 convert_reduce_fusion.2
  308.7 1.3 fusion.39
  310.1 24.9 %reduce-scatter.16.cloned.1.call-done = bf16[128,1024]{1,0:T(8,128)(2,1)} async-done(((bf16[512,1024]{1,0:T(8,128)(2,1)}), bf16[128,1024]{1,0:T(8,128)(2,1)}) %reduce-scatter.16.cloned.1.call-update) | async-done | bytes 262160 | tf_op jit(solution)/shard_map/reduce_scatter | solution.py:117
  334.9 2.1 fusion.52
  337.8 16.8 %all-gather.21.cloned.1.call-done = bf16[512,1024]{1,0:T(8,128)(2,1)} async-done(((bf16[128,1024]{1,0:T(8,128)(2,1)}), bf16[512,1024]{1,0:T(8,128)(2,1)}) %all-gather.21.cloned.1.call-update) | async-done | bytes 1048592 | tf_op jit(solution)/shard_map/all_gather | solution.py:161
  354.7 1.7 convolution_convert_fusion.3
  356.4 3.2 convert_reduce_fusion.5
  360.9 1.2 multiply_convert_fusion
  362.9 1.2 convert_reduce_fusion.6
  366.1 3.0 bitcast_convert_fusion
  370.0 24.1 %reduce-scatter.20.cloned.1.call-done = bf16[128,1024]{1,0:T(8,128)(2,1)} async-done(((bf16[512,1024]{1,0:T(8,128)(2,1)}), bf16[128,1024]{1,0:T(8,128)(2,1)}) %reduce-scatter.20.cloned.1.call-update) | async-done | bytes 262160 | tf_op jit(solution)/shard_map/reduce_scatter | solution.py:206
  394.1 1.2 convert_reduce_fusion.1
  395.3 1.3 fusion.40
  397.4 1.4 fusion.58
  398.9 5.4 fusion.50
  405.8 3.3 fusion.59
  410.4 2.8 fusion.21
  415.0 43.1 %reduce-scatter.32.cloned.1.call-done = f32[32,4]{1,0:T(8,128)} async-done(((f32[256,4]{1,0:T(8,128)}), f32[32,4]{1,0:T(8,128)}) %reduce-scatter.32.cloned.1.call-update) | async-done | bytes 528
  458.2 1.4 copy.85
  459.6 19.5 %all-reduce = f32[2,4,64]{2,1,0:T(4,128)S(1)} all-reduce(f32[2,4,64]{2,1,0:T(4,128)S(1)} %pad_maximum_fusion.3), channel_id=8, replica_groups=mesh['dp'=8,'tensor'=4] {'dp'}, use_global_device_ids=true, to_apply=%region_28.29.clone | all-reduce | flops 512 | bytes 4096
  480.7 33.3 %reduce-scatter.22.cloned.1.call-done = f32[6,128]{1,0:T(8,128)} async-done(((f32[6,1024]{1,0:T(8,128)}), f32[6,128]{1,0:T(8,128)}) %reduce-scatter.22.cloned.1.call-update) | async-done | bytes 3088 | tf_op jit(solution)/shard_map/reduce_scatter | solution.py:234
  513.9 6.3 psum.7
  520.3 60.5 %reduce-scatter.26.cloned.1.call-done = f32[256,128]{1,0:T(8,128)} async-done(((f32[256,1024]{1,0:T(8,128)}), f32[256,128]{1,0:T(8,128)}) %reduce-scatter.26.cloned.1.call-update) | async-done | bytes 131088 | tf_op jit(solution)/shard_map/reduce_scatter | solution.py:230
  580.8 91.8 %reduce-scatter.30.cloned.1.call-done = f32[1024,128]{1,0:T(8,128)} async-done(((f32[1024,1024]{1,0:T(8,128)}), f32[1024,128]{1,0:T(8,128)}) %reduce-scatter.30.cloned.1.call-update) | async-done | bytes 524304 | tf_op jit(solution)/shard_map/reduce_scatter | solution.py:233
  672.6 91.8 %reduce-scatter.28.cloned.1.call-done = f32[128,1024]{1,0:T(8,128)} async-done(((f32[1024,1024]{1,0:T(8,128)}), f32[128,1024]{1,0:T(8,128)}) %reduce-scatter.28.cloned.1.call-update) | async-done | bytes 524304 | tf_op jit(solution)/shard_map/reduce_scatter | solution.py:231
  764.4 79.2 %reduce-scatter.24.cloned.1.call-done = f32[128,3,256]{2,0,1:T(8,128)} async-done(((f32[1024,3,256]{2,0,1:T(8,128)}), f32[128,3,256]{2,0,1:T(8,128)}) %reduce-scatter.24.cloned.1.call-update) | async-done | bytes 393232 | tf_op jit(solution)/shard_map/reduce_scatter | solution.py:228
  (116 shorter events, 26.6 us)
Async XLA Ops:
  7.2 67.2 %copy-start.13 = (bf16[256,128]{1,0:T(8,128)(2,1)S(1)}, bf16[256,128]{1,0:T(8,128)(2,1)}, u32[]{:S(2)}) copy-start(bf16[256,128]{1,0:T(8,128)(2,1)} %param.16) | copy-start | bytes 196612
  7.2 94.4 %all-gather.11.cloned.1.call-start = ((), (), s32[]{:S(2)}) async-start(), calls=%async_computation.11 | async-start | bytes 1769472 | tf_op jit(solution)/shard_map/all_gather | solution.py:49
  7.9 95.5 %all-gather.9.cloned.1.call-start = ((), (), s32[]{:S(2)}) async-start(), calls=%async_computation.10 | async-start | bytes 1310720 | tf_op jit(solution)/shard_map/all_gather | solution.py:72
  40.7 94.5 %reduce-scatter.14.cloned.1.call-start = ((), (), s32[]{:S(2)}) async-start(), calls=%async_computation.12 | async-start | bytes 1310720 | tf_op jit(solution)/shard_map/reduce_scatter | solution.py:104
  105.6 1.2 copy-start.9
  108.3 1.9 copy-start
  111.1 24.2 %copy-start.2 = (bf16[128,1024]{1,0:T(8,128)(2,1)S(1)}, bf16[128,1024]{1,0:T(8,128)(2,1)}, u32[]{:S(2)}) copy-start(bf16[128,1024]{1,0:T(8,128)(2,1)} %param.10) | copy-start | bytes 786436
  112.6 28.2 %copy-start.14 = (f32[4,32]{1,0:T(4,128)S(1)}, f32[4,32]{1,0:T(4,128)}, u32[]{:S(2)}) copy-start(f32[4,32]{1,0:T(4,128)} %param.18) | copy-start | bytes 1540
  112.6 74.3 %all-gather.15.cloned.1.call-start = ((), (), s32[]{:S(2)}) async-start(), calls=%async_computation.14 | async-start | bytes 2359296 | tf_op jit(solution)/shard_map/all_gather | solution.py:54
  113.2 91.0 %all-gather.13.cloned.1.call-start = ((), (), s32[]{:S(2)}) async-start(), calls=%async_computation.13 | async-start | bytes 1310720 | tf_op jit(solution)/shard_map/all_gather | solution.py:112
  139.4 83.0 %all-gather.19.cloned.1.call-start = ((), (), s32[]{:S(2)}) async-start(), calls=%async_computation.17 | async-start | bytes 1310720 | tf_op jit(solution)/shard_map/all_gather | solution.py:132
  140.0 135.7 %all-gather.17.cloned.1.call-start = ((), (), s32[]{:S(2)}) async-start(), calls=%async_computation.15 | async-start | bytes 2359296 | tf_op jit(solution)/shard_map/all_gather | solution.py:58
  140.8 166.7 %reduce-scatter.18.cloned.1.call-start = ((), (), s32[]{:S(2)}) async-start(), calls=%async_computation.18 | async-start | bytes 1310720 | tf_op jit(solution)/shard_map/reduce_scatter | solution.py:149
  275.8 6.2 copy-start.15
  280.9 1.0 copy-start.10
  284.3 23.2 %copy-start.3 = (bf16[128,1024]{1,0:T(8,128)(2,1)S(1)}, bf16[128,1024]{1,0:T(8,128)(2,1)}, u32[]{:S(2)}) copy-start(bf16[128,1024]{1,0:T(8,128)(2,1)} %reduce-scatter.14.cloned.1.call-done) | copy-start | bytes 786436
  284.3 50.7 %reduce-scatter.16.cloned.1.call-start = ((), (), s32[]{:S(2)}) async-start(), calls=%async_computation.16 | async-start | bytes 1310720 | tf_op jit(solution)/shard_map/reduce_scatter | solution.py:117
  289.2 45.7 %copy-start.7 = (bf16[128,1024]{1,0:T(8,128)(2,1)S(1)}, bf16[128,1024]{1,0:T(8,128)(2,1)}, u32[]{:S(2)}) copy-start(bf16[128,1024]{1,0:T(8,128)(2,1)} %param.11) | copy-start | bytes 786436
  289.3 65.4 %all-gather.21.cloned.1.call-start = ((), (), s32[]{:S(2)}) async-start(), calls=%async_computation.19 | async-start | bytes 1310720 | tf_op jit(solution)/shard_map/all_gather | solution.py:161
  337.8 56.4 %reduce-scatter.20.cloned.1.call-start = ((), (), s32[]{:S(2)}) async-start(), calls=%async_computation.20 | async-start | bytes 1310720 | tf_op jit(solution)/shard_map/reduce_scatter | solution.py:206
  356.4 3.5 copy-start.1
  362.9 3.3 copy-start.6
  369.1 28.3 %copy-start.8 = (bf16[512,1024]{1,0:T(8,128)(2,1)S(1)}, bf16[512,1024]{1,0:T(8,128)(2,1)}, u32[]{:S(2)}) copy-start(bf16[512,1024]{1,0:T(8,128)(2,1)} %all-gather.21.cloned.1.call-done) | copy-start | bytes 3145732
  369.1 89.1 %reduce-scatter.32.cloned.1.call-start = ((), (), s32[]{:S(2)}) async-start(), calls=%async_computation.26 | async-start | bytes 147456
  370.0 143.9 %reduce-scatter.22.cloned.1.call-start = ((), (), s32[]{:S(2)}) async-start(), calls=%async_computation.21 | async-start | bytes 36864 | tf_op jit(solution)/shard_map/reduce_scatter | solution.py:234
  397.3 183.5 %reduce-scatter.26.cloned.1.call-start = ((), (), s32[]{:S(2)}) async-start(), calls=%async_computation.23 | async-start | bytes 1179648 | tf_op jit(solution)/shard_map/reduce_scatter | solution.py:230
  398.8 273.8 %reduce-scatter.30.cloned.1.call-start = ((), (), s32[]{:S(2)}) async-start(), calls=%async_computation.25 | async-start | bytes 4718592 | tf_op jit(solution)/shard_map/reduce_scatter | solution.py:233
  404.3 1.2 copy-start.5
  404.3 1.5 copy-start.11
  404.3 360.1 %reduce-scatter.28.cloned.1.call-start = ((), (), s32[]{:S(2)}) async-start(), calls=%async_computation.24 | async-start | bytes 4718592 | tf_op jit(solution)/shard_map/reduce_scatter | solution.py:231
  409.1 1.0 copy-start.12
  409.1 1.3 copy-start.16
  409.1 434.5 %reduce-scatter.24.cloned.1.call-start = ((), (), s32[]{:S(2)}) async-start(), calls=%async_computation.22 | async-start | bytes 3538944 | tf_op jit(solution)/shard_map/reduce_scatter | solution.py:228
  413.2 0.7 copy-start.17
  413.2 66.5 %copy-start.4 = (bf16[128,1024]{1,0:T(8,128)(2,1)S(1)}, bf16[128,1024]{1,0:T(8,128)(2,1)}, u32[]{:S(2)}) copy-start(bf16[128,1024]{1,0:T(8,128)(2,1)} %reduce-scatter.20.cloned.1.call-done) | copy-start | bytes 786436
Sparse Core Ops, SparseCore 0:
  10.2 47.1 all-gather.10
  59.5 15.5 all-gather.8
  112.7 22.5 reduce-scatter.13
  137.5 49.3 all-gather.14
  188.9 15.1 all-gather.12
  205.6 16.7 all-gather.18
  224.6 51.0 all-gather.16
  284.4 23.0 reduce-scatter.17
  310.0 24.8 reduce-scatter.15
  337.9 16.7 all-gather.20
  369.2 24.8 reduce-scatter.19
  397.3 60.8 reduce-scatter.31
  461.3 52.5 reduce-scatter.21
  517.8 62.9 reduce-scatter.25
  585.3 87.2 reduce-scatter.29
  676.7 87.6 reduce-scatter.27
  768.8 74.7 reduce-scatter.23
where the time goes:
time: 851 us; the launch traced here: 850 us
  waiting for transfers between devices  618 us (73%)
  blocking collectives  132 us (16%)
  matrix products  46.4 us (5%)
  other arithmetic  22.6 us (3%)
  local copies, waits for them, and re-layouts  15.4 us (2%)
  between operations  14.9 us (2%)
    reduce_scatter x1, waiting for transfers between devices, on_device(): lax.psum_scatter(grad_down, 'dp', scatter_dimension=1, tiled=True)  91.8 us
    reduce_scatter x1, waiting for transfers between devices, on_device(): lax.psum_scatter(grad_up, 'dp', scatter_dimension=0, tiled=True)  91.8 us
    reduce_scatter x1, waiting for transfers between devices, on_device(): lax.psum_scatter(grad_qkv, 'dp', scatter_dimension=0, tiled=True)  79.2 us
    reduce_scatter x1, waiting for transfers between devices, on_device(): lax.psum_scatter(grad_weight, 'dp', scatter_dimension=1, tiled=True)  60.5 us
    all_gather x1, waiting for transfers between devices, on_device(): lax.all_gather(w_down, 'dp', axis=1, tiled=True)  53.4 us
    unnamed x18, waiting for transfers between devices  45.8 us
    reduce_scatter x1, waiting for transfers between devices, on_device(): lax.psum_scatter(grad_vecs, 'dp', scatter_dimension=1, tiled=True)  33.3 us
    all_gather x1, blocking collectives, on_device(): lax.all_gather(qv_bias.astype(jnp.bfloat16), 'dp', axis=2, tiled=True)  30.5 us
  transfers between devices with their start and end apart: 17, of which 15 were waited for; matrix products, arithmetic and copies ran while one was open for 5% of the time, Pallas kernels for 0%

commit v1 on v0

--- a/solution.py
+++ b/solution.py
@@ -1,6 +1,8 @@
 import jax
 import jax.numpy as jnp
 from jax import lax
+from jax.experimental import pallas as pl
+from jax.experimental.pallas import tpu as pltpu
 from jax.sharding import PartitionSpec as P
 
 epsilon = 1e-05
@@ -247,9 +249,615 @@
     )
 
 
+Z_COUNT, Y_COUNT, T_COUNT = 4, 2, 4
+MESH_ID = pl.DeviceIdType.MESH
+ANYWHERE = pl.BlockSpec(memory_space=pl.ANY)
+IN_VMEM = pl.BlockSpec(memory_space=pltpu.VMEM)
+
+
+class Place:
+    def __init__(self):
+        dp = lax.axis_index("dp")
+        self.t = lax.axis_index("tensor")
+        self.z = dp // Y_COUNT
+        self.y = dp % Y_COUNT
+        self.other_y = 1 - self.y
+        self.dp = dp
+
+    def owner(self, z_index, y_index):
+        return z_index * Y_COUNT + y_index
+
+    def z_next(self, step):
+        return lax.rem(self.z + step, Z_COUNT)
+
+    def z_prev(self, step):
+        return lax.rem(self.z + Z_COUNT - step, Z_COUNT)
+
+    def z_peer(self, step):
+        return (self.owner(self.z_next(step), self.y), self.t)
+
+    def y_peer(self):
+        return (self.owner(self.z, self.other_y), self.t)
+
+    def t_next(self, step):
+        return lax.rem(self.t + step, T_COUNT)
+
+    def t_peer(self, step):
+        return (self.dp, self.t_next(step))
+
+    def barrier(self):
+        sem = pltpu.get_barrier_semaphore()
+        peers = [self.z_peer(k) for k in range(1, Z_COUNT)]
+        peers += [self.y_peer()]
+        peers += [self.t_peer(k) for k in range(1, T_COUNT)]
+        for peer in peers:
+            pl.semaphore_signal(sem, inc=1, device_id=peer, device_id_type=MESH_ID)
+        pl.semaphore_wait(sem, len(peers))
+
+
+def block_of(ref, owner, size, axis):
+    start = pl.multiple_of(owner * size, size)
+    if axis == 0:
+        return ref.at[pl.ds(start, size), :]
+    return ref.at[:, pl.ds(start, size)]
+
+
+def remote(src, dst, send_sem, recv_sem, peer):
+    return pltpu.make_async_remote_copy(
+        src_ref=src,
+        dst_ref=dst,
+        send_sem=send_sem,
+        recv_sem=recv_sem,
+        device_id=peer,
+        device_id_type=MESH_ID,
+    )
+
+
+class DpGather:
+    def __init__(self, here, shard, full, axis, sems):
+        self.here, self.shard, self.full, self.axis = here, shard, full, axis
+        self.send, self.recv, self.own = sems
+        self.size = shard.shape[axis]
+        self.flights = []
+
+    def slot(self, owner):
+        return block_of(self.full, owner, self.size, self.axis)
+
+    def start(self):
+        here = self.here
+        mine = self.slot(here.dp)
+        self.local = pltpu.make_async_copy(self.shard, mine, self.own)
+        self.local.start()
+        self.z_flights = []
+        self.y_flights = [remote(self.shard, mine, self.send.at[3], self.recv.at[3], here.y_peer())]
+        self.y_flights[0].start()
+        for k in range(1, Z_COUNT):
+            flight = remote(self.shard, mine, self.send.at[k - 1], self.recv.at[k - 1], here.z_peer(k))
+            flight.start()
+            self.z_flights.append(flight)
+
+    def forward(self):
+        here = self.here
+        for k in range(1, Z_COUNT):
+            self.z_flights[k - 1].wait_recv()
+            held = self.slot(here.owner(here.z_prev(k), here.y))
+            flight = remote(held, held, self.send.at[3 + k], self.recv.at[3 + k], here.y_peer())
+            flight.start()
+            self.y_flights.append(flight)
+
+    def finish(self):
+        for flight in self.y_flights:
+            flight.wait_recv()
+        for flight in self.z_flights + self.y_flights:
+            flight.wait_send()
+        self.local.wait()
+
+
+class DpScatter:
+    def __init__(self, here, part, total, axis, y_buf, z_out, z_in, sems):
+        self.here, self.part, self.total, self.axis = here, part, total, axis
+        self.y_buf, self.z_out, self.z_in = y_buf, z_out, z_in
+        self.send, self.recv = sems
+        self.size = total.shape[axis]
+
+    def slot(self, owner):
+        return block_of(self.part, owner, self.size, self.axis)
+
+    def start(self):
+        here = self.here
+        self.y_flights = {}
+        for k in (1, 2, 3, 0):
+            src = self.slot(here.owner(here.z_next(k), here.other_y))
+            flight = remote(src, self.y_buf.at[k], self.send.at[k], self.recv.at[k], here.y_peer())
+            flight.start()
+            self.y_flights[k] = flight
+
+    def middle(self):
+        here = self.here
+        self.z_flights = []
+        for k in range(1, Z_COUNT):
+            self.y_flights[k].wait_recv()
+            own = self.slot(here.owner(here.z_next(k), here.y))[...]
+            both = own.astype(jnp.float32) + self.y_buf[k].astype(jnp.float32)
+            self.z_out[k - 1] = both.astype(self.z_out.dtype)
+            flight = remote(
+                self.z_out.at[k - 1],
+                self.z_in.at[k - 1],
+                self.send.at[3 + k],
+                self.recv.at[3 + k],
+                here.z_peer(k),
+            )
+            flight.start()
+            self.z_flights.append(flight)
+
+    def finish(self):
+        self.y_flights[0].wait_recv()
+        own = self.slot(self.here.dp)[...].astype(jnp.float32)
+        acc = own + self.y_buf[0].astype(jnp.float32)
+        for k in range(1, Z_COUNT):
+            self.z_flights[k - 1].wait_recv()
+            acc = acc + self.z_in[k - 1].astype(jnp.float32)
+        self.total[...] = acc
+        for flight in list(self.y_flights.values()) + self.z_flights:
+            flight.wait_send()
+
+
+class TensorGather:
+    def __init__(self, here, full, rows, send, recv):
+        self.here, self.full, self.rows = here, full, rows
+        self.send, self.recv = send, recv
+
+    def start(self, src=None):
+        here = self.here
+        mine = block_of(self.full, here.t, self.rows, 0)
+        self.flights = []
+        for k in (2, 3, 1):
+            flight = remote(
+                mine if src is None else src,
+                mine,
+                self.send.at[k - 1],
+                self.recv.at[k - 1],
+                here.t_peer(k),
+            )
+            flight.start()
+            self.flights.append(flight)
+
+    def finish(self):
+        for flight in self.flights:
+            flight.wait_recv()
+        for flight in self.flights:
+            flight.wait_send()
+
+
+class TensorScatter:
+    def __init__(self, here, part, buf, send, recv):
+        self.here, self.part, self.buf = here, part, buf
+        self.send, self.recv = send, recv
+        self.rows = buf.shape[1]
+
+    def start(self):
+        here = self.here
+        self.flights = []
+        for k in (2, 3, 1):
+            flight = remote(
+                block_of(self.part, here.t_next(k), self.rows, 0),
+                self.buf.at[k - 1],
+                self.send.at[k - 1],
+                self.recv.at[k - 1],
+                here.t_peer(k),
+            )
+            flight.start()
+            self.flights.append(flight)
+
+    def total(self):
+        for flight in self.flights:
+            flight.wait_recv()
+        acc = block_of(self.part, self.here.t, self.rows, 0)[...].astype(jnp.float32)
+        for k in range(T_COUNT - 1):
+            acc = acc + self.buf[k].astype(jnp.float32)
+        return acc
+
+    def finish(self):
+        for flight in self.flights:
+            flight.wait_send()
+
+
+DMA = pltpu.SemaphoreType.DMA
+gather_sems = [DMA((7,)), DMA((7,)), DMA]
+pair_sems = [DMA((7,)), DMA((7,))]
+tensor_sems = [DMA((3,)), DMA((3,))]
+
+
+def scatter_scratch(block, dtype):
+    return [
+        pltpu.VMEM((4,) + block, dtype),
+        pltpu.VMEM((3,) + block, dtype),
+        pltpu.VMEM((3,) + block, dtype),
+    ] + pair_sems
+
+
+def call(kernel, name, outs, in_specs, out_specs, scratch, collective_id):
+    return pl.pallas_call(
+        kernel,
+        name=name,
+        out_shape=outs,
+        in_specs=in_specs,
+        out_specs=out_specs,
+        scratch_shapes=scratch,
+        compiler_params=pltpu.CompilerParams(
+            collective_id=collective_id,
+            has_side_effects=True,
+            vmem_limit_bytes=44 * 1024 * 1024,
+        ),
+    )
+
+
+def gather_kernel(
+    tok, cot, small, qkv, out, up, tok_full, cot_full, small_full, qkv_full, out_full, up_full, *sems
+):
+    here = Place()
+    here.barrier()
+    rows = tok.shape[0]
+    shards = (
+        (small, small_full, 0),
+        (qkv, qkv_full, 0),
+        (out, out_full, 1),
+        (up, up_full, 0),
+    )
+    gathers = [
+        DpGather(here, shard, full, axis, sems[3 * i : 3 * i + 3])
+        for i, (shard, full, axis) in enumerate(shards)
+    ]
+    rest = sems[3 * len(shards) :]
+    across = []
+    for i, (own, full) in enumerate(((tok, tok_full), (cot, cot_full))):
+        local = pltpu.make_async_copy(own, block_of(full, here.t, rows, 0), rest[4 + i])
+        local.start()
+        moving = TensorGather(here, full, rows, rest[2 * i], rest[2 * i + 1])
+        moving.start(own)
+        across.append((local, moving))
+    for item in gathers:
+        item.start()
+    for item in gathers:
+        item.forward()
+    for item in gathers:
+        item.finish()
+    for local, moving in across:
+        moving.finish()
+        local.wait()
+
+
+def normalize(values):
+    center = values - jnp.mean(values, axis=-1, keepdims=True)
+    scale = lax.rsqrt(jnp.mean(center * center, axis=-1, keepdims=True) + epsilon)
+    return center * scale, scale
+
+
+def middle_kernel(
+    part, tok, vec, down, mid, normed_full, down_full, buf, g_send, g_recv, g_own, s_send, s_recv, a_send, a_recv
+):
+    here = Place()
+    here.barrier()
+    scatter = TensorScatter(here, part, buf, s_send, s_recv)
+    scatter.start()
+    weights = DpGather(here, down, down_full, 1, (g_send, g_recv, g_own))
+    weights.start()
+    rows = tok.shape[0]
+    middle = tok[...].astype(jnp.float32) + scatter.total() + vec[2:3]
+    mid[...] = middle
+    hat, _ = normalize(middle)
+    block_of(normed_full, here.t, rows, 0)[...] = (hat * vec[3:4] + vec[4:5]).astype(jnp.bfloat16)
+    spread = TensorGather(here, normed_full, rows, a_send, a_recv)
+    spread.start()
+    weights.forward()
+    spread.finish()
+    weights.finish()
+    scatter.finish()
+
+
+def norm_back(grad, values, gain):
+    hat, scale = normalize(values)
+    e = grad * gain
+    inner = scale * (
+        e - jnp.mean(e, axis=-1, keepdims=True) - hat * jnp.mean(e * hat, axis=-1, keepdims=True)
+    )
+    gain_grad = jnp.sum(grad * hat, axis=0, keepdims=True)
+    shift_grad = jnp.sum(grad, axis=0, keepdims=True)
+    return inner, gain_grad, shift_grad
+
+
+def back_kernel(
+    part_mlp, part_norm, mid, cot, vec, grad_down, result, grad_mid, attn_full, sums, total_down,
+    buf_norm, buf_mlp, y_buf, z_out, z_in, d_send, d_recv, n_send, n_recv, m_send, m_recv, a_send, a_recv
+):
+    here = Place()
+    here.barrier()
+    rows = mid.shape[0]
+    first = TensorScatter(here, part_norm, buf_norm, n_send, n_recv)
+    first.start()
+    second = TensorScatter(here, part_mlp, buf_mlp, m_send, m_recv)
+    second.start()
+    down = DpScatter(here, grad_down, total_down, 1, y_buf, z_out, z_in, (d_send, d_recv))
+    down.start()
+    grad_out = cot[...].astype(jnp.float32)
+    inner, gain_grad, shift_grad = norm_back(first.total(), mid[...], vec[3:4])
+    grad = grad_out + inner
+    grad_mid[...] = grad
+    block_of(attn_full, here.t, rows, 0)[...] = grad.astype(jnp.bfloat16)
+    spread = TensorGather(here, attn_full, rows, a_send, a_recv)
+    spread.start()
+    zero = jnp.zeros_like(gain_grad)
+    sums[0:1] = zero
+    sums[1:2] = zero
+    sums[2:3] = jnp.sum(grad, axis=0, keepdims=True)
+    sums[3:4] = gain_grad
+    sums[4:5] = shift_grad
+    sums[5:6] = jnp.sum(grad_out, axis=0, keepdims=True)
+    sums[6:7] = zero
+    sums[7:8] = zero
+    result[...] = (mid[...] + second.total() + vec[5:6]).astype(jnp.bfloat16)
+    down.middle()
+    spread.finish()
+    down.finish()
+    first.finish()
+    second.finish()
+
+
+def last_kernel(
+    part, tok, grad_mid, vec, sums, bias_rows, grad_out, grad_up, grad_qkv,
+    grad_tok, total_small, total_out, total_up, total_qkv,
+    buf, small_part, small_mine, small_sum, small_buf, t_send, t_recv, v_send, v_recv, *scratch
+):
+    here = Place()
+    here.barrier()
+    scatter = TensorScatter(here, part, buf, t_send, t_recv)
+    scatter.start()
+    plan = ((grad_out, total_out, 1), (grad_up, total_up, 0), (grad_qkv, total_qkv, 0))
+    big = []
+    for i, (ref, total, axis) in enumerate(plan):
+        group = scratch[5 * i : 5 * i + 5]
+        item = DpScatter(here, ref, total, axis, *group[:3], group[3:])
+        item.start()
+        big.append(item)
+    inner, gain_grad, shift_grad = norm_back(
+        scatter.total(), tok[...].astype(jnp.float32), vec[0:1]
+    )
+    grad_tok[...] = (grad_mid[...] + inner).astype(jnp.bfloat16)
+    width = total_small.shape[1]
+    for d in range(Z_COUNT * Y_COUNT):
+        cols = slice(d * width, (d + 1) * width)
+        small_part[8 * d : 8 * d + 8] = sums[:, cols] + bias_rows[8 * d : 8 * d + 8]
+        small_part[8 * d : 8 * d + 1] = gain_grad[:, cols]
+        small_part[8 * d + 1 : 8 * d + 2] = shift_grad[:, cols]
+    group = scratch[15:20]
+    small = DpScatter(here, small_part, small_mine, 0, *group[:3], group[3:])
+    small.start()
+    big[0].middle()
+    small.middle()
+    big[1].middle()
+    big[2].middle()
+    small.finish()
+    small_sum[...] = small_mine[...]
+    flights = []
+    for k in range(1, T_COUNT):
+        flight = remote(
+            small_sum, small_buf.at[k - 1], v_send.at[k - 1], v_recv.at[k - 1], here.t_peer(k)
+        )
+        flight.start()
+        flights.append(flight)
+    for item in big:
+        item.finish()
+    for flight in flights:
+        flight.wait_recv()
+    everyone = small_mine[...] + small_buf[0] + small_buf[1] + small_buf[2]
+    row = lax.broadcasted_iota(jnp.int32, everyone.shape, 0)
+    total_small[...] = jnp.where(row < 6, everyone, small_mine[...])
+    for flight in flights:
+        flight.wait_send()
+    scatter.finish()
+
+
+def on_device_direct(
+    tokens, cotangent, seg_lengths, vectors, w_qkv, qv_bias, w_out, w_up, up_bias, w_down
+):
+    bf16, f32 = jnp.bfloat16, jnp.float32
+    rows, width = tokens.shape
+    heads, head_part = qv_bias.shape[1], qv_bias.shape[2]
+    dp, cols = Z_COUNT * Y_COUNT, vectors.shape[1]
+    head_size = head_part * dp
+    group_size = rows * T_COUNT
+    local_width = w_qkv.shape[2]
+    hidden = w_up.shape[1]
+    up_part = up_bias.shape[1]
+    lengths = seg_lengths[0]
+    shape = jax.ShapeDtypeStruct
+    qkv_wide = 3 * local_width
+    qv_row = jnp.pad(qv_bias.reshape(1, -1), ((0, 0), (0, cols - qv_bias.size)))
+    small = jnp.concatenate(
+        [vectors, qv_row, up_bias.reshape(1, cols), jnp.zeros((8, cols), f32)]
+    ).astype(bf16)
+    tok_full, cot_full, small_full, qkv_full, out_full, up_full = call(
+        gather_kernel,
+        "gather_inputs",
+        [
+            shape((group_size, width), bf16),
+            shape((group_size, width), bf16),
+            shape((dp * 16, cols), bf16),
+            shape((width, qkv_wide), bf16),
+            shape((local_width, width), bf16),
+            shape((width, hidden), bf16),
+        ],
+        [ANYWHERE] * 6,
+        [ANYWHERE] * 6,
+        gather_sems * 4 + tensor_sems * 2 + [DMA, DMA],
+        1,
+    )(tokens, cotangent, small, w_qkv.reshape(-1, qkv_wide), w_out, w_up)
+    small_full = small_full.reshape(dp, 16, cols).astype(f32)
+    vec_full = small_full[:, :8].transpose(1, 0, 2).reshape(8, width)
+    bias_full = (
+        small_full[:, 6, : qv_bias.size]
+        .reshape(dp, 2, heads, head_part)
+        .transpose(1, 2, 0, 3)
+        .reshape(2, local_width)
+    )
+    upbias_full = small_full[:, 7].reshape(dp, heads, up_part).transpose(1, 0, 2).reshape(hidden)
+
+    head_ids = lax.axis_index("tensor") * heads + jnp.arange(heads, dtype=jnp.int32)
+    slopes = jnp.exp2(-8.0 * (head_ids + 1).astype(f32) / (heads * T_COUNT))
+    group_one = layer_norm(tok_full.astype(f32), vec_full[0], vec_full[1]).astype(bf16)
+    projected = jnp.dot(group_one, qkv_full, preferred_element_type=f32)
+    projected = projected.reshape(group_size, 3, local_width)
+    head_shape = (group_size, heads, head_size)
+    query_heads = (projected[:, 0] + bias_full[0]).astype(bf16).reshape(head_shape)
+    key_heads = projected[:, 1].astype(bf16).reshape(head_shape)
+    value_heads = (projected[:, 2] + bias_full[1]).astype(bf16).reshape(head_shape)
+    scores = block_scores(query_heads, key_heads, 0, slopes, lengths)
+    row_max = jnp.max(scores, axis=-1, keepdims=True)
+    exponent = jnp.exp(scores - row_max)
+    row_sum = jnp.sum(exponent, axis=-1, keepdims=True)
+    probs = exponent / row_sum
+    weights = probs.astype(bf16)
+    attended = (
+        jnp.einsum("hqk,khd->qhd", weights, value_heads, preferred_element_type=f32)
+        .reshape(group_size, local_width)
+        .astype(bf16)
+    )
+    part_attn = jnp.dot(attended, out_full, preferred_element_type=f32).astype(bf16)
+
+    middle, group_two, down_full = call(
+        middle_kernel,
+        "middle",
+        [
+            shape((rows, width), f32),
+            shape((group_size, width), bf16),
+            shape((hidden, width), bf16),
+        ],
+        [IN_VMEM, IN_VMEM, IN_VMEM, ANYWHERE],
+        [IN_VMEM, IN_VMEM, ANYWHERE],
+        [pltpu.VMEM((3, rows, width), bf16)] + gather_sems + tensor_sems * 2,
+        2,
+    )(part_attn, tokens, vec_full, w_down)
+
+    contract_rows = (((0,), (0,)), ((), ()))
+    contract_cols = (((1,), (1,)), ((), ()))
+    pre_act = jnp.dot(group_two, up_full, preferred_element_type=f32) + upbias_full
+    activated, gelu_back = jax.vjp(gelu_tanh, pre_act)
+    activated = activated.astype(bf16)
+    part_mlp = jnp.dot(activated, down_full, preferred_element_type=f32).astype(bf16)
+    grad_act = lax.dot_general(cot_full, down_full, contract_cols, preferred_element_type=f32)
+    grad_pre = gelu_back(grad_act)[0].astype(bf16)
+    part_norm = lax.dot_general(
+        grad_pre, up_full, contract_cols, preferred_element_type=f32
+    ).astype(bf16)
+    grad_down = lax.dot_general(
+        activated, cot_full, contract_rows, preferred_element_type=f32
+    ).astype(bf16)
+    grad_up = lax.dot_general(
+        group_two, grad_pre, contract_rows, preferred_element_type=f32
+    ).astype(bf16)
+    grad_upbias = jnp.sum(grad_pre.astype(f32), axis=0)
+
+    output, grad_middle, attn_full, sums, total_down = call(
+        back_kernel,
+        "back",
+        [
+            shape((rows, width), bf16),
+            shape((rows, width), f32),
+            shape((group_size, width), bf16),
+            shape((8, width), f32),
+            shape((hidden, cols), f32),
+        ],
+        [IN_VMEM] * 6,
+        [IN_VMEM] * 5,
+        [pltpu.VMEM((3, rows, width), bf16)] * 2
+        + scatter_scratch((hidden, cols), bf16)
+        + tensor_sems * 3,
+        3,
+    )(part_mlp, part_norm, middle, cotangent, vec_full, grad_down)
+
+    grad_out = lax.dot_general(
+        attended, attn_full, contract_rows, preferred_element_type=f32
+    ).astype(bf16)
+    grad_heads = (
+        lax.dot_general(attn_full, out_full, contract_cols, preferred_element_type=f32)
+        .astype(bf16)
+        .reshape(head_shape)
+    )
+    score_scale = head_size ** (-0.5)
+    grad_probs = jnp.einsum("qhd,khd->hqk", grad_heads, value_heads, preferred_element_type=f32)
+    row_term = jnp.sum(probs * grad_probs, axis=-1, keepdims=True)
+    grad_scores = (probs * (grad_probs - row_term)).astype(bf16)
+    grad_query = (
+        jnp.einsum("hqk,khd->qhd", grad_scores, key_heads, preferred_element_type=f32) * score_scale
+    )
+    grad_keys = (
+        jnp.einsum("hqk,qhd->khd", grad_scores, query_heads, preferred_element_type=f32)
+        * score_scale
+    )
+    grad_values = jnp.einsum("hqk,qhd->khd", weights, grad_heads, preferred_element_type=f32)
+    grad_proj = jnp.concatenate(
+        [item.reshape(group_size, local_width).astype(bf16) for item in (grad_query, grad_keys, grad_values)],
+        axis=1,
+    )
+    bias_sums = jnp.sum(grad_proj.astype(f32), axis=0)
+    grad_qvbias = jnp.stack([bias_sums[:local_width], bias_sums[2 * local_width :]])
+    grad_qkv = lax.dot_general(
+        group_one, grad_proj, contract_rows, preferred_element_type=f32
+    ).astype(bf16)
+    part_first = lax.dot_general(
+        grad_proj, qkv_full, contract_cols, preferred_element_type=f32
+    ).astype(bf16)
+    qv_rows = (
+        grad_qvbias.reshape(2, heads, dp, head_part).transpose(2, 0, 1, 3).reshape(dp, 1, qv_bias.size)
+    )
+    qv_rows = jnp.pad(qv_rows, ((0, 0), (0, 0), (0, cols - qv_bias.size)))
+    up_rows = grad_upbias.reshape(heads, dp, up_part).transpose(1, 0, 2).reshape(dp, 1, cols)
+    bias_rows = jnp.concatenate([jnp.zeros((dp, 6, cols), f32), qv_rows, up_rows], axis=1)
+    bias_rows = bias_rows.reshape(dp * 8, cols)
+
+    grad_tokens, total_small, total_out, total_up, total_qkv = call(
+        last_kernel,
+        "last",
+        [
+            shape((rows, width), bf16),
+            shape((8, cols), f32),
+            shape((local_width, cols), f32),
+            shape((width // dp, hidden), f32),
+            shape((width // dp, qkv_wide), f32),
+        ],
+        [IN_VMEM] * 9,
+        [IN_VMEM] * 5,
+        [
+            pltpu.VMEM((3, rows, width), bf16),
+            pltpu.VMEM((8 * dp, cols), f32),
+            pltpu.VMEM((8, cols), f32),
+            pltpu.VMEM((8, cols), f32),
+            pltpu.VMEM((3, 8, cols), f32),
+        ]
+        + tensor_sems * 2
+        + scatter_scratch((local_width, cols), bf16)
+        + scatter_scratch((width // dp, hidden), bf16)
+        + scatter_scratch((width // dp, qkv_wide), bf16)
+        + scatter_scratch((8, cols), f32),
+        4,
+    )(part_first, tokens, grad_middle, vec_full, sums, bias_rows, grad_out, grad_up, grad_qkv)
+    return (
+        output,
+        grad_tokens,
+        total_small[:6],
+        total_qkv.reshape(w_qkv.shape),
+        total_small[6, : qv_bias.size].reshape(qv_bias.shape),
+        total_out,
+        total_up,
+        total_small[7].reshape(up_bias.shape),
+        total_down,
+    )
+
+
 def solution(mesh):
+    direct = mesh.shape["dp"] == Z_COUNT * Y_COUNT and mesh.shape["tensor"] == T_COUNT
     return jax.shard_map(
-        on_device,
+        on_device_direct if direct else on_device,
         mesh=mesh,
         in_specs=(
             P(("dp", "tensor"), None),

time: 851 us -> 306 us (0.36)
  waiting for transfers between devices: 618 us -> 0 us
  Pallas kernels: 0 us -> 237 us
  blocking collectives: 132 us -> 0 us
  other arithmetic: 22.6 us -> 7.81 us
  between operations: 14.9 us -> 1.3 us
    reduce_scatter x9 -> x0, waiting for transfers between devices: 446 us -> none  [the longest x1 91.8 us: on_device(): lax.psum_scatter(grad_down, 'dp', scatter_dimension=1, tiled=True)]
    pallas_call x0 -> x4, Pallas kernels: none -> 237 us  [the longest x1 95.9 us: on_device_direct(): call(last_kernel, 'last', [shape((rows, width), bf16), shape((8, cols), f...]
    all_gather x7 -> x0, waiting for transfers between devices: 127 us -> none  [the longest x1 53.4 us: on_device(): lax.all_gather(w_down, 'dp', axis=1, tiled=True)]
    all_gather x4 -> x0, blocking collectives: 106 us -> none  [the longest x1 30.5 us: on_device(): lax.all_gather(qv_bias.astype(jnp.bfloat16), 'dp', axis=2, tiled=True)]
    unnamed x18 -> x0, waiting for transfers between devices: 45.8 us -> none
    unnamed x1 -> x0, blocking collectives: 19.5 us -> none
    dot_general x18 -> x17, matrix products: 46.4 us -> 36 us  [the longest x1 4.51 us: on_device_direct(): jnp.einsum('hqk,qhd->khd', weights, grad_heads, preferred_element_type=f32)]
  transfers between devices with their start and end apart: 17 -> 0, of which waited for: 15 -> 0; matrix products, arithmetic and copies ran while one was open for 5% -> 0% of each run, Pallas kernels for 0% -> 0%
where the time goes in v1:
time: 306 us; the launch traced here: 304 us
  Pallas kernels  237 us (77%)
  matrix products  41.3 us (13%)
  local copies, waits for them, and re-layouts  16.6 us (5%)
  other arithmetic  7.81 us (3%)
    pallas_call x1, Pallas kernels, on_device_direct(): call(last_kernel, 'last', [shape((rows, width), bf16), shape((8, cols), f...  95.9 us
    pallas_call x1, Pallas kernels, on_device_direct(): call(gather_kernel, 'gather_inputs', [shape((group_size, width), bf16), s...  61.9 us
    pallas_call x1, Pallas kernels, on_device_direct(): call(back_kernel, 'back', [shape((rows, width), bf16), shape((rows, width...  42.5 us
    pallas_call x1, Pallas kernels, on_device_direct(): call(middle_kernel, 'middle', [shape((rows, width), f32), shape((group_si...  36.6 us
    unnamed x86, local copies, waits for them, and re-layouts  10.5 us

profile of v1, /device:TPU:0, one launch (start us, length us, event | category | flops | bytes accessed | tf_op | source)
XLA Modules:
  0.0 303.8 jit_solution(16230536409561798382)
XLA Ops:
  0.6 0.7 convert.20
  1.4 0.7 convert.21
  2.2 0.7 convert.19
  3.0 1.1 copy.58
  4.3 0.9 copy-done
  5.2 0.9 copy-done.2
  6.2 0.9 copy-done.13
  7.1 0.8 copy-done.14
  8.0 61.9 %gather_inputs.1 = (bf16[512,1024]{1,0:T(8,128)(2,1)S(1)}, bf16[512,1024]{1,0:T(8,128)(2,1)S(1)}, bf16[128,128]{1,0:T(8,128)(2,1)S(1)}, bf16[1024,768]{1,0:T(8,1...) custom-call(bf16[128,1024]{1,0:T(8,128)(2,1)S(1)} %copy-done, ...), custom_call_target="tpu_custom_call" | custom-call | tf_op jit(solution)/shard_map/gather_inputs/pallas_call | solution.py:679
  69.9 0.2 convert_reduce_fusion
  70.2 0.4 fusion.4
  70.6 2.4 fusion.36
  73.0 2.1 fusion.39
  75.3 1.2 subtract_convert_fusion
  76.4 0.2 reduce-window.8
  76.7 0.9 fusion.24
  77.8 1.2 slice.93
  79.0 5.3 %fusion.43 = (f32[4,512]{1,0:T(4,128)S(1)}, f32[4,512,512]{1,2,0:T(8,128)}) fusion(f32[512,512]{0,1:T(8,128)} %subtract_convert_fusion, f32[4]{0:T(128)S(1)} %multiply_exponential_fusion, pred[512,512]{0,1:T(8,128)(4,1)} %fusion.24, bf16[512,4,64]{0,2,1:T(8,128)(2,1)S(1)} %add_convert_fusion, bf16[512,4,64]{0,2,1:T(8,128)(2,1)S(1)} %bitcast.89), kind=kOutput, calls=%fused_computation.85 | convolution fusion | flops 140509696 | bytes 6037520 | tf_op jit(solution)/shard_map/sub | solution.py:716
  84.3 3.9 %convolution_convert_fusion.10 = bf16[4,64,512]{2,1,0:T(8,128)(2,1)S(1)} fusion(f32[512,4,64]{0,2,1:T(8,128)} %bitcast.94, f32[4,64]{1,0:T(4,128)S(1)} %add.86, f32[4,512]{1,0:T(4,128)S(1)} %get-tuple-element.95, f32[512,512]{0,1:T(8,128)} %subtract_convert_fusion, f32[4]{0:T(128)S(1)} %multiply_exponential_fusion, pred[512,512]{0,1:T(8,128)(4,1)} %fusion.24, ...), kind=kOutput, calls=%fused_computation.44 | convolution fusion | flops 276171264 | bytes 2630672 | tf_op jit(solution)/shard_map/hqk,khd->qhd/dot_general | solution.py:721
  88.3 0.5 convolution_convert_fusion.6.part
  88.7 36.6 %middle.1 = (f32[128,1024]{1,0:T(8,128)S(1)}, bf16[512,1024]{1,0:T(8,128)(2,1)S(1)}, bf16[1024,1024]{1,0:T(8,128)(2,1)S(1)}) custom-call(bf16[512,1024]{1,0:T(8,128)(2,1)S(1)} %convolution_convert_fusion.6.part, bf16[128,1024]{1,0:T(8,128)(2,1)S(1)} %copy-done.1, f32[8,1024]{1,0:T(8,128)S(1)} %get-tuple-element.87.vec, bf16[1024,128]{1,0:T(8,128)(2,1)S(1)} %copy-done.10), custom_call_target="tpu_custom_call" | custom-call | tf_op jit(solution)/shard_map/middle/pallas_call | solution.py:727
  125.4 2.6 fusion.44
  128.2 3.9 %convolution_convert_fusion.5.part_mlp = bf16[512,1024]{1,0:T(8,128)(2,1)S(1)} fusion(bf16[1024,1024]{1,0:T(8,128)(2,1)} %copy-done.18, f32[512,1024]{1,0:T(8,128)} %fusion.44, f32[1024]{0:T(1024)S(1)} %add.95), kind=kOutput, calls=%fused_computation.37 | convolution fusion | flops 1079508992 | bytes 5246976 | tf_op jit(solution)/shard_map/dot_general | solution.py:746
  132.2 2.7 convert_reduce_fusion.1
  134.9 1.3 convolution_convert_fusion.4.part_norm
  136.2 1.6 convolution_convert_fusion.1.grad_down
  137.8 42.5 %back.1 = (bf16[128,1024]{1,0:T(8,128)(2,1)S(1)}, f32[128,1024]{1,0:T(8,128)S(1)}, bf16[512,1024]{1,0:T(8,128)(2,1)S(1)}, f32[8,1024]{1,0:T(8,128)S(1)}, f32[1024,128]{1,0:T(8,128)S(1)}) custom-call(bf16[512,1024]{1,0:T(8,128)(2,1)S(1)} %convolution_convert_fusion.5.part_mlp, bf16[512,1024]{1,0:T(8,128)(2,1)S(1)} %convolution_convert_fusion.4.part_norm, ...), custom_call_target="tpu_custom_call" | custom-call | tf_op jit(solution)/shard_map/back/pallas_call | solution.py:760
  180.4 1.2 convolution_convert_fusion.9
  181.6 4.5 %convolution_convert_fusion.8 = bf16[4,64,512]{2,1,0:T(8,128)(2,1)} fusion(bf16[512,4,64]{0,2,1:T(8,128)(2,1)} %bitcast.111, f32[4,512]{1,0:T(4,128)S(1)} %get-tuple-element.95, f32[512,512]{0,1:T(8,128)} %subtract_convert_fusion, f32[4]{0:T(128)S(1)} %multiply_exponential_fusion, pred[512,512]{0,1:T(8,128)(4,1)} %fusion.24, ...), kind=kOutput, calls=%fused_computation.42 | convolution fusion | flops 275909120 | bytes 2367504 | tf_op jit(solution)/shard_map/hqk,qhd->khd/dot_general | solution.py:797
  186.1 3.4 %multiply_reduce_fusion = (f32[4,512]{1,0:T(4,128)S(1)}, f32[4,512,512]{1,2,0:T(8,128)S(1)}) fusion(f32[4,512,512]{1,2,0:T(8,128)} %get-tuple-element.96, f32[4,512]{1,0:T(4,128)S(1)} %get-tuple-element.95, bf16[512,4,64]{0,2,1:T(8,128)(2,1)} %bitcast.112, f32[512,4,64]{0,2,1:T(8,128)S(1)} %bitcast.95, f32[4,64]{1,0:T(4,128)S(1)} %add.86), kind=kOutput, calls=%fused_computation.2 | convolution fusion | flops 137623552 | bytes 9192448 | tf_op jit(solution)/shard_map/qhd,khd->hqk/dot_general | solution.py:787
  189.6 1.2 multiply_convert_fusion
  190.8 0.8 fusion.21
  191.8 0.5 fusion.20
  192.3 1.0 convolution_convert_fusion.3.part
  193.5 1.3 convert_reduce_fusion.2
  195.2 1.4 convolution_convert_fusion.7.grad_out
  196.7 3.1 %convolution_convert_fusion.grad_up = bf16[1024,1024]{1,0:T(8,128)(2,1)S(1)} fusion(bf16[512,1024]{1,0:T(8,128)(2,1)} %copy-done.22, bf16[512,1024]{1,0:T(8,128)(2,1)} %copy-done.38), kind=kOutput, calls=%fused_computation.31 | convolution fusion | flops 1074790400 | bytes 4194304 | tf_op jit(solution)/shard_map/dot_general | solution.py:755
  199.9 1.3 convolution_convert_fusion.2.grad_qkv
  201.2 95.9 %last.1 = (bf16[128,1024]{1,0:T(8,128)(2,1)S(1)}, f32[8,128]{1,0:T(8,128)S(1)}, f32[256,128]{1,0:T(8,128)S(1)}, f32[128,1024]{1,0:T(8,128)S(1)}, f32[128,768]{1,0:T(8,128)S(1)}) custom-call(bf16[512,1024]{1,0:T(8,128)(2,1)S(1)} %convolution_convert_fusion.3.part, bf16[128,1024]{1,0:T(8,128)(2,1)S(1)} %copy-done.1, f32[128,1024]{1,0:T(8,128)S(1)} %copy-done.5, ...), custom_call_target="tpu_custom_call" | custom-call | tf_op jit(solution)/shard_map/last/pallas_call | solution.py:818
  297.2 0.9 copy.74
  298.1 0.7 reshape_squeeze.14
  298.9 0.7 reshape_squeeze.15
  299.5 0.7 copy.87
  300.2 0.7 copy.88
  300.9 0.6 copy.89
  301.5 0.7 copy.90
  302.2 0.8 copy.91
  303.0 0.8 copy.92
  (115 shorter events, 2.4 us)
Async XLA Ops:
  4.3 1.0 copy-start
  5.2 0.9 copy-start.2
  6.2 0.9 copy-start.13
  7.1 0.8 copy-start.14
  69.9 3.1 %copy-start.15 = (bf16[1024,1024]{1,0:T(8,128)(2,1)}, bf16[1024,1024]{1,0:T(8,128)(2,1)S(1)}, u32[]{:S(2)}) copy-start(bf16[1024,1024]{1,0:T(8,128)(2,1)S(1)} %get-tuple-element.33) | copy-start | bytes 6291460
  69.9 3.1 %copy-start.20 = (bf16[1024,768]{1,0:T(8,128)(2,1)}, bf16[1024,768]{1,0:T(8,128)(2,1)S(1)}, u32[]{:S(2)}) copy-start(bf16[1024,768]{1,0:T(8,128)(2,1)S(1)} %get-tuple-element.30) | copy-start | bytes 4718596
  73.0 3.5 %copy-start.36 = (s32[1,4]{1,0:T(1,128)S(1)}, s32[1,4]{1,0:T(1,128)}, u32[]{:S(2)}) copy-start(s32[1,4]{1,0:T(1,128)} %param.12) | copy-start | bytes 52
  77.8 6.5 %copy-start.25 = (bf16[512,4,64]{0,2,1:T(8,128)(2,1)}, bf16[512,4,64]{0,2,1:T(8,128)(2,1)S(1)}, u32[]{:S(2)}) copy-start(bf16[512,4,64]{0,2,1:T(8,128)(2,1)S(1)} %add_convert_fusion) | copy-start | bytes 786436
  79.0 5.3 %copy-start.31 = (bf16[512,1,256]{0,2,1:T(8,128)(2,1)}, bf16[512,1,256]{0,2,1:T(8,128)(2,1)S(1)}, u32[]{:S(2)}) copy-start(bf16[512,1,256]{0,2,1:T(8,128)(2,1)S(1)} %slice.93) | copy-start | bytes 786436
  84.3 4.4 %copy-start.1 = (bf16[128,1024]{1,0:T(8,128)(2,1)S(1)}, bf16[128,1024]{1,0:T(8,128)(2,1)}, u32[]{:S(2)}) copy-start(bf16[128,1024]{1,0:T(8,128)(2,1)} %tok.5) | copy-start | bytes 786436
  84.3 4.4 %copy-start.10 = (bf16[1024,128]{1,0:T(8,128)(2,1)S(1)}, bf16[1024,128]{1,0:T(8,128)(2,1)}, u32[]{:S(2)}) copy-start(bf16[1024,128]{1,0:T(8,128)(2,1)} %down.1) | copy-start | bytes 786436
  88.2 39.8 %copy-start.24 = (bf16[4,64,512]{2,1,0:T(8,128)(2,1)}, bf16[4,64,512]{2,1,0:T(8,128)(2,1)S(1)}, u32[]{:S(2)}) copy-start(bf16[4,64,512]{2,1,0:T(8,128)(2,1)S(1)} %convolution_convert_fusion.10) | copy-start | bytes 786436
  88.3 37.1 %copy-start.16 = (bf16[1024,1024]{1,0:T(8,128)(2,1)S(1)}, bf16[1024,1024]{1,0:T(8,128)(2,1)}, u32[]{:S(2)}) copy-start(bf16[1024,1024]{1,0:T(8,128)(2,1)} %copy-done.15) | copy-start | bytes 6291460
  125.4 2.7 copy-start.6
  125.4 2.7 copy-start.18
  125.4 2.7 copy-start.22
  128.2 3.9 %copy-start.19 = (bf16[1024,1024]{1,0:T(8,128)(2,1)S(1)}, bf16[1024,1024]{1,0:T(8,128)(2,1)}, u32[]{:S(2)}) copy-start(bf16[1024,1024]{1,0:T(8,128)(2,1)} %copy-done.18) | copy-start | bytes 6291460
  128.2 3.9 %copy-start.37 = (f32[512,1024]{1,0:T(8,128)S(1)}, f32[512,1024]{1,0:T(8,128)}, u32[]{:S(2)}) copy-start(f32[512,1024]{1,0:T(8,128)} %fusion.44) | copy-start | bytes 6291460
  132.1 2.7 copy-start.17
  134.8 1.3 copy-start.38
  136.2 1.7 copy-start.3
  136.2 1.7 copy-start.7
  180.3 1.2 copy-start.8
  180.3 1.2 copy-start.11
  180.3 5.7 %copy-start.4 = (f32[128,1024]{1,0:T(8,128)}, f32[128,1024]{1,0:T(8,128)S(1)}, u32[]{:S(2)}) copy-start(f32[128,1024]{1,0:T(8,128)S(1)} %get-tuple-element.39.grad_mid) | copy-start | bytes 1572868
  181.6 4.5 %copy-start.33 = (f32[512,1,256]{0,2,1:T(8,128)S(1)}, f32[512,1,256]{0,2,1:T(8,128)}, u32[]{:S(2)}) copy-start(f32[512,1,256]{0,2,1:T(8,128)} %get-tuple-element.86) | copy-start | bytes 1572868
  186.1 3.5 %copy-start.23 = (f32[4,512,512]{1,2,0:T(8,128)S(1)}, f32[4,512,512]{1,2,0:T(8,128)}, u32[]{:S(2)}) copy-start(f32[4,512,512]{1,2,0:T(8,128)} %get-tuple-element.96) | copy-start | bytes 12582916
  189.6 1.2 copy-start.26
  190.8 1.0 copy-start.32
  190.8 1.5 copy-start.21
  190.8 1.5 copy-start.34
  191.6 1.8 copy-start.27
  192.2 1.1 copy-start.29
  196.6 3.2 %copy-start.28 = (bf16[4,64,512]{2,1,0:T(8,128)(2,1)S(1)}, bf16[4,64,512]{2,1,0:T(8,128)(2,1)}, u32[]{:S(2)}) copy-start(bf16[4,64,512]{2,1,0:T(8,128)(2,1)} %copy-done.27) | copy-start | bytes 786436
  196.6 3.2 %copy-start.30 = (bf16[4,64,512]{2,1,0:T(8,128)(2,1)S(1)}, bf16[4,64,512]{2,1,0:T(8,128)(2,1)}, u32[]{:S(2)}) copy-start(bf16[4,64,512]{2,1,0:T(8,128)(2,1)} %copy-done.29) | copy-start | bytes 786436
  196.7 3.2 %copy-start.35 = (bf16[4,64,512]{2,1,0:T(8,128)(2,1)S(1)}, bf16[4,64,512]{2,1,0:T(8,128)(2,1)}, u32[]{:S(2)}) copy-start(bf16[4,64,512]{2,1,0:T(8,128)(2,1)} %convolution_convert_fusion.8) | copy-start | bytes 786436
  199.9 1.3 copy-start.5
  201.2 98.4 %copy-start.12 = (bf16[128,1024]{1,0:T(8,128)(2,1)S(1)}, bf16[128,1024]{1,0:T(8,128)(2,1)}, u32[]{:S(2)}) copy-start(bf16[128,1024]{1,0:T(8,128)(2,1)} %copy-done.11) | copy-start | bytes 786436
  297.0 5.9 %copy-start.9 = (f32[1024,128]{1,0:T(8,128)S(1)}, f32[1024,128]{1,0:T(8,128)}, u32[]{:S(2)}) copy-start(f32[1024,128]{1,0:T(8,128)} %copy-done.8) | copy-start | bytes 1572868

commit v2 on v1

--- a/solution.py
+++ b/solution.py
@@ -287,7 +287,7 @@
 
     def barrier(self):
         sem = pltpu.get_barrier_semaphore()
-        peers = [self.z_peer(k) for k in range(1, Z_COUNT)]
+        peers = [self.z_peer(1), self.z_peer(Z_COUNT - 1)]
         peers += [self.y_peer()]
         peers += [self.t_peer(k) for k in range(1, T_COUNT)]
         for peer in peers:
@@ -318,32 +318,30 @@
         self.here, self.shard, self.full, self.axis = here, shard, full, axis
         self.send, self.recv, self.own = sems
         self.size = shard.shape[axis]
-        self.flights = []
 
     def slot(self, owner):
         return block_of(self.full, owner, self.size, self.axis)
+
+    def fly(self, src, dst, index, peer):
+        flight = remote(src, dst, self.send.at[index], self.recv.at[index], peer)
+        flight.start()
+        return flight
 
     def start(self):
         here = self.here
         mine = self.slot(here.dp)
+        self.z_flights = [self.fly(self.shard, mine, 0, here.z_peer(1))]
+        self.y_flights = [self.fly(self.shard, mine, 3, here.y_peer())]
         self.local = pltpu.make_async_copy(self.shard, mine, self.own)
         self.local.start()
-        self.z_flights = []
-        self.y_flights = [remote(self.shard, mine, self.send.at[3], self.recv.at[3], here.y_peer())]
-        self.y_flights[0].start()
-        for k in range(1, Z_COUNT):
-            flight = remote(self.shard, mine, self.send.at[k - 1], self.recv.at[k - 1], here.z_peer(k))
-            flight.start()
-            self.z_flights.append(flight)
-
-    def forward(self):
+
+    def step(self, k):
         here = self.here
-        for k in range(1, Z_COUNT):
-            self.z_flights[k - 1].wait_recv()
-            held = self.slot(here.owner(here.z_prev(k), here.y))
-            flight = remote(held, held, self.send.at[3 + k], self.recv.at[3 + k], here.y_peer())
-            flight.start()
-            self.y_flights.append(flight)
+        self.z_flights[k - 1].wait_recv()
+        held = self.slot(here.owner(here.z_prev(k), here.y))
+        if k < Z_COUNT - 1:
+            self.z_flights.append(self.fly(held, held, k, here.z_peer(1)))
+        self.y_flights.append(self.fly(held, held, 3 + k, here.y_peer()))
 
     def finish(self):
         for flight in self.y_flights:
@@ -359,46 +357,40 @@
         self.y_buf, self.z_out, self.z_in = y_buf, z_out, z_in
         self.send, self.recv = sems
         self.size = total.shape[axis]
+        self.y_flights, self.z_flights = [], []
 
     def slot(self, owner):
         return block_of(self.part, owner, self.size, self.axis)
 
-    def start(self):
+    def fly(self, src, dst, index, peer):
+        flight = remote(src, dst, self.send.at[index], self.recv.at[index], peer)
+        flight.start()
+        return flight
+
+    def send_y(self, k):
         here = self.here
-        self.y_flights = {}
-        for k in (1, 2, 3, 0):
-            src = self.slot(here.owner(here.z_next(k), here.other_y))
-            flight = remote(src, self.y_buf.at[k], self.send.at[k], self.recv.at[k], here.y_peer())
-            flight.start()
-            self.y_flights[k] = flight
-
-    def middle(self):
+        src = self.slot(here.owner(here.z_prev(k), here.other_y))
+        self.y_flights.append(self.fly(src, self.y_buf.at[k - 1], k - 1, here.y_peer()))
+
+    def sum(self, k):
         here = self.here
-        self.z_flights = []
-        for k in range(1, Z_COUNT):
-            self.y_flights[k].wait_recv()
-            own = self.slot(here.owner(here.z_next(k), here.y))[...]
-            both = own.astype(jnp.float32) + self.y_buf[k].astype(jnp.float32)
-            self.z_out[k - 1] = both.astype(self.z_out.dtype)
-            flight = remote(
-                self.z_out.at[k - 1],
-                self.z_in.at[k - 1],
-                self.send.at[3 + k],
-                self.recv.at[3 + k],
-                here.z_peer(k),
-            )
-            flight.start()
-            self.z_flights.append(flight)
+        self.y_flights[k - 1].wait_recv()
+        own = self.slot(here.owner(here.z_prev(k), here.y))[...].astype(jnp.float32)
+        acc = own + self.y_buf[k - 1].astype(jnp.float32)
+        if k > 1:
+            self.z_flights[k - 2].wait_recv()
+            acc = acc + self.z_in[k - 2].astype(jnp.float32)
+        return acc
+
+    def step(self, k):
+        self.z_out[k - 1] = self.sum(k).astype(self.z_out.dtype)
+        self.z_flights.append(
+            self.fly(self.z_out.at[k - 1], self.z_in.at[k - 1], 3 + k, self.here.z_peer(1))
+        )
 
     def finish(self):
-        self.y_flights[0].wait_recv()
-        own = self.slot(self.here.dp)[...].astype(jnp.float32)
-        acc = own + self.y_buf[0].astype(jnp.float32)
-        for k in range(1, Z_COUNT):
-            self.z_flights[k - 1].wait_recv()
-            acc = acc + self.z_in[k - 1].astype(jnp.float32)
-        self.total[...] = acc
-        for flight in list(self.y_flights.values()) + self.z_flights:
+        self.total[...] = self.sum(Z_COUNT)
+        for flight in self.y_flights + self.z_flights:
             flight.wait_send()
 
 
@@ -518,8 +510,9 @@
         across.append((local, moving))
     for item in gathers:
         item.start()
-    for item in gathers:
-        item.forward()
+    for k in range(1, Z_COUNT):
+        for item in gathers:
+            item.step(k)
     for item in gathers:
         item.finish()
     for local, moving in across:
@@ -542,6 +535,7 @@
     scatter.start()
     weights = DpGather(here, down, down_full, 1, (g_send, g_recv, g_own))
     weights.start()
+    weights.step(1)
     rows = tok.shape[0]
     middle = tok[...].astype(jnp.float32) + scatter.total() + vec[2:3]
     mid[...] = middle
@@ -549,7 +543,8 @@
     block_of(normed_full, here.t, rows, 0)[...] = (hat * vec[3:4] + vec[4:5]).astype(jnp.bfloat16)
     spread = TensorGather(here, normed_full, rows, a_send, a_recv)
     spread.start()
-    weights.forward()
+    weights.step(2)
+    weights.step(3)
     spread.finish()
     weights.finish()
     scatter.finish()
@@ -567,18 +562,20 @@
 
 
 def back_kernel(
-    part_mlp, part_norm, mid, cot, vec, grad_down, result, grad_mid, attn_full, sums, total_down,
-    buf_norm, buf_mlp, y_buf, z_out, z_in, d_send, d_recv, n_send, n_recv, m_send, m_recv, a_send, a_recv
+    part_norm, mid, cot, vec, grad_down, grad_mid, attn_full, sums, total_down,
+    buf_norm, y_buf, z_out, z_in, d_send, d_recv, n_send, n_recv, a_send, a_recv
 ):
     here = Place()
     here.barrier()
     rows = mid.shape[0]
     first = TensorScatter(here, part_norm, buf_norm, n_send, n_recv)
     first.start()
-    second = TensorScatter(here, part_mlp, buf_mlp, m_send, m_recv)
-    second.start()
     down = DpScatter(here, grad_down, total_down, 1, y_buf, z_out, z_in, (d_send, d_recv))
-    down.start()
+    down.send_y(1)
+    down.send_y(2)
+    down.step(1)
+    down.send_y(3)
+    down.send_y(4)
     grad_out = cot[...].astype(jnp.float32)
     inner, gain_grad, shift_grad = norm_back(first.total(), mid[...], vec[3:4])
     grad = grad_out + inner
@@ -586,6 +583,7 @@
     block_of(attn_full, here.t, rows, 0)[...] = grad.astype(jnp.bfloat16)
     spread = TensorGather(here, attn_full, rows, a_send, a_recv)
     spread.start()
+    down.step(2)
     zero = jnp.zeros_like(gain_grad)
     sums[0:1] = zero
     sums[1:2] = zero
@@ -595,30 +593,36 @@
     sums[5:6] = jnp.sum(grad_out, axis=0, keepdims=True)
     sums[6:7] = zero
     sums[7:8] = zero
-    result[...] = (mid[...] + second.total() + vec[5:6]).astype(jnp.bfloat16)
-    down.middle()
+    down.step(3)
     spread.finish()
     down.finish()
     first.finish()
-    second.finish()
 
 
 def last_kernel(
-    part, tok, grad_mid, vec, sums, bias_rows, grad_out, grad_up, grad_qkv,
-    grad_tok, total_small, total_out, total_up, total_qkv,
-    buf, small_part, small_mine, small_sum, small_buf, t_send, t_recv, v_send, v_recv, *scratch
+    part, part_mlp, tok, mid, grad_mid, vec, sums, bias_rows, grad_out, grad_up, grad_qkv,
+    grad_tok, result, total_small, total_out, total_up, total_qkv,
+    buf, buf_mlp, small_part, small_mine, small_sum, small_buf,
+    t_send, t_recv, m_send, m_recv, v_send, v_recv, *scratch
 ):
     here = Place()
     here.barrier()
-    scatter = TensorScatter(here, part, buf, t_send, t_recv)
-    scatter.start()
     plan = ((grad_out, total_out, 1), (grad_up, total_up, 0), (grad_qkv, total_qkv, 0))
     big = []
     for i, (ref, total, axis) in enumerate(plan):
         group = scratch[5 * i : 5 * i + 5]
         item = DpScatter(here, ref, total, axis, *group[:3], group[3:])
-        item.start()
+        item.send_y(1)
         big.append(item)
+    scatter = TensorScatter(here, part, buf, t_send, t_recv)
+    scatter.start()
+    second = TensorScatter(here, part_mlp, buf_mlp, m_send, m_recv)
+    second.start()
+    for item in big:
+        item.send_y(2)
+    for item in big:
+        item.step(1)
+        item.send_y(3)
     inner, gain_grad, shift_grad = norm_back(
         scatter.total(), tok[...].astype(jnp.float32), vec[0:1]
     )
@@ -631,11 +635,17 @@
         small_part[8 * d + 1 : 8 * d + 2] = shift_grad[:, cols]
     group = scratch[15:20]
     small = DpScatter(here, small_part, small_mine, 0, *group[:3], group[3:])
-    small.start()
-    big[0].middle()
-    small.middle()
-    big[1].middle()
-    big[2].middle()
+    for k in range(1, Z_COUNT + 1):
+        small.send_y(k)
+    for item in big:
+        item.step(2)
+        item.send_y(4)
+    small.step(1)
+    result[...] = (mid[...] + second.total() + vec[5:6]).astype(jnp.bfloat16)
+    small.step(2)
+    for item in big:
+        item.step(3)
+    small.step(3)
     small.finish()
     small_sum[...] = small_mine[...]
     flights = []
@@ -655,6 +665,7 @@
     for flight in flights:
         flight.wait_send()
     scatter.finish()
+    second.finish()
 
 
 def on_device_direct(
@@ -757,23 +768,22 @@
     ).astype(bf16)
     grad_upbias = jnp.sum(grad_pre.astype(f32), axis=0)
 
-    output, grad_middle, attn_full, sums, total_down = call(
+    grad_middle, attn_full, sums, total_down = call(
         back_kernel,
         "back",
         [
-            shape((rows, width), bf16),
             shape((rows, width), f32),
             shape((group_size, width), bf16),
             shape((8, width), f32),
             shape((hidden, cols), f32),
         ],
-        [IN_VMEM] * 6,
         [IN_VMEM] * 5,
-        [pltpu.VMEM((3, rows, width), bf16)] * 2
+        [IN_VMEM] * 4,
+        [pltpu.VMEM((3, rows, width), bf16)]
         + scatter_scratch((hidden, cols), bf16)
-        + tensor_sems * 3,
+        + tensor_sems * 2,
         3,
-    )(part_mlp, part_norm, middle, cotangent, vec_full, grad_down)
+    )(part_norm, middle, cotangent, vec_full, grad_down)
 
     grad_out = lax.dot_general(
         attended, attn_full, contract_rows, preferred_element_type=f32
@@ -815,32 +825,34 @@
     bias_rows = jnp.concatenate([jnp.zeros((dp, 6, cols), f32), qv_rows, up_rows], axis=1)
     bias_rows = bias_rows.reshape(dp * 8, cols)
 
-    grad_tokens, total_small, total_out, total_up, total_qkv = call(
+    grad_tokens, output, total_small, total_out, total_up, total_qkv = call(
         last_kernel,
         "last",
         [
+            shape((rows, width), bf16),
             shape((rows, width), bf16),
             shape((8, cols), f32),
             shape((local_width, cols), f32),
             shape((width // dp, hidden), f32),
             shape((width // dp, qkv_wide), f32),
         ],
-        [IN_VMEM] * 9,
-        [IN_VMEM] * 5,
+        [IN_VMEM] * 11,
+        [IN_VMEM] * 6,
         [
+            pltpu.VMEM((3, rows, width), bf16),
             pltpu.VMEM((3, rows, width), bf16),
             pltpu.VMEM((8 * dp, cols), f32),
             pltpu.VMEM((8, cols), f32),
             pltpu.VMEM((8, cols), f32),
             pltpu.VMEM((3, 8, cols), f32),
         ]
-        + tensor_sems * 2
+        + tensor_sems * 3
         + scatter_scratch((local_width, cols), bf16)
         + scatter_scratch((width // dp, hidden), bf16)
         + scatter_scratch((width // dp, qkv_wide), bf16)
         + scatter_scratch((8, cols), f32),
         4,
-    )(part_first, tokens, grad_middle, vec_full, sums, bias_rows, grad_out, grad_up, grad_qkv)
+    )(part_first, part_mlp, tokens, middle, grad_middle, vec_full, sums, bias_rows, grad_out, grad_up, grad_qkv)
     return (
         output,
         grad_tokens,

time: 306 us -> 240 us (0.78)
  Pallas kernels: 237 us -> 168 us
  local copies, waits for them, and re-layouts: 16.6 us -> 24.2 us
    pallas_call x2, Pallas kernels: 138 us -> 84.1 us  [the longest x1 54.5 us: on_device_direct(): call(last_kernel, 'last', [shape((rows, width), bf16), shape((rows, width...]
    unnamed x86 -> x90, local copies, waits for them, and re-layouts: 10.5 us -> 19.5 us
    pallas_call x1, Pallas kernels: 61.9 us -> 53 us  [on_device_direct(): call(gather_kernel, 'gather_inputs', [shape((group_size, width), bf16), s...]
    pallas_call x1, Pallas kernels: 36.6 us -> 31 us  [on_device_direct(): call(middle_kernel, 'middle', [shape((rows, width), f32), shape((group_si...]
where the time goes in v2:
time: 240 us
  Pallas kernels  168 us (70%)
  matrix products  39.2 us (16%)
  local copies, waits for them, and re-layouts  24.2 us (10%)
  other arithmetic  6.74 us (3%)
    pallas_call x1, Pallas kernels, on_device_direct(): call(last_kernel, 'last', [shape((rows, width), bf16), shape((rows, width...  54.5 us
    pallas_call x1, Pallas kernels, on_device_direct(): call(gather_kernel, 'gather_inputs', [shape((group_size, width), bf16), s...  53 us
    pallas_call x1, Pallas kernels, on_device_direct(): call(middle_kernel, 'middle', [shape((rows, width), f32), shape((group_si...  31 us
    pallas_call x1, Pallas kernels, on_device_direct(): call(back_kernel, 'back', [shape((rows, width), f32), shape((group_size,...  29.6 us
    unnamed x90, local copies, waits for them, and re-layouts  19.5 us
    sub x1, matrix products, on_device_direct(): exponent = jnp.exp(scores - row_max)  5.27 us

profile of v2, /device:TPU:0, one launch (start us, length us, event | category | flops | bytes accessed | tf_op | source)
XLA Modules:
  0.0 239.6 jit_solution(8337407285418702134)
XLA Ops:
  0.7 0.9 reduce-window.8
  1.7 0.7 convert.21
  2.5 0.7 convert.19
  3.2 0.7 convert.20
  4.1 1.1 copy.58
  5.6 1.2 subtract_convert_fusion
  6.8 53.0 %gather_inputs.1 = (bf16[512,1024]{1,0:T(8,128)(2,1)S(1)}, bf16[512,1024]{1,0:T(8,128)(2,1)S(1)}, bf16[128,128]{1,0:T(8,128)(2,1)S(1)}, bf16[1024,768]{1,0:T(8,1...) custom-call(bf16[128,1024]{1,0:T(8,128)(2,1)S(1)} %copy-done, ...), custom_call_target="tpu_custom_call" | custom-call | tf_op jit(solution)/shard_map/gather_inputs/pallas_call | solution.py:690
  59.9 1.0 copy-done.25
  63.1 2.6 %fusion.36 = f32[512,768]{0,1:T(8,128)S(1)} fusion(bf16[1024,768]{1,0:T(8,128)(2,1)} %copy-done.23, bf16[512,1024]{1,0:T(8,128)(2,1)S(1)} %get-tuple-element.28, f32[1024]{0:T(1024)S(1)} %bitcast.109, f32[1024]{0:T(1024)S(1)} %bitcast.107, f32[512]{0:T(512)S(1)} %add_rsqrt_fusion, f32[512]{0:T(512)S(1)} %broadcast_multiply_fusion), kind=kOutput, calls=%fused_computation.80 | convolution fusion | flops 808452096 | bytes 4206592 | tf_op jit(solution)/shard_map/dot_general | solution.py:719
  65.8 0.9 fusion.39
  66.8 5.3 %fusion.43 = (f32[4,512]{1,0:T(4,128)S(1)}, f32[4,512,512]{1,2,0:T(8,128)}) fusion(f32[512,512]{0,1:T(8,128)} %subtract_convert_fusion, f32[4]{0:T(128)S(1)} %multiply_exponential_fusion, pred[512,512]{0,1:T(8,128)(4,1)S(1)} %fusion.24, bf16[512,4,64]{0,2,1:T(8,128)(2,1)S(1)} %add_convert_fusion.1, bf16[512,4,64]{0,2,1:T(8,128)(2,1)S(1)} %bitcast.91), kind=kOutput, calls=%fused_computation.85 | convolution fusion | flops 140509696 | bytes 6037520 | tf_op jit(solution)/shard_map/sub | solution.py:727
  72.1 3.7 %convolution_convert_fusion.10 = bf16[4,64,512]{2,1,0:T(8,128)(2,1)S(1)} fusion(f32[512,4,64]{0,2,1:T(8,128)S(1)} %bitcast.96, f32[4,64]{1,0:T(4,128)S(1)} %add.92, f32[4,512]{1,0:T(4,128)S(1)} %get-tuple-element.95, f32[512,512]{0,1:T(8,128)} %subtract_convert_fusion, f32[4]{0:T(128)S(1)} %multiply_exponential_fusion, pred[512,512]{0,1:T(8,128)(4,1)} %copy-done.38, ...), kind=kOutput, calls=%fused_computation.44 | convolution fusion | flops 276171264 | bytes 2630672 | tf_op jit(solution)/shard_map/hqk,khd->qhd/dot_general | solution.py:732
  76.3 31.0 %middle.1 = (f32[128,1024]{1,0:T(8,128)S(1)}, bf16[512,1024]{1,0:T(8,128)(2,1)}, bf16[1024,1024]{1,0:T(8,128)(2,1)S(1)}) custom-call(bf16[512,1024]{1,0:T(8,128)(2,1)S(1)} %convolution_convert_fusion.6.part, bf16[128,1024]{1,0:T(8,128)(2,1)S(1)} %copy-done, f32[8,1024]{1,0:T(8,128)S(1)} %get-tuple-element.87.vec, bf16[1024,128]{1,0:T(8,128)(2,1)S(1)} %copy-done.13), custom_call_target="tpu_custom_call" | custom-call | tf_op jit(solution)/shard_map/middle/pallas_call | solution.py:738
  107.3 2.7 %fusion.44 = f32[512,1024]{1,0:T(8,128)S(1)} fusion(bf16[512,1024]{1,0:T(8,128)(2,1)} %get-tuple-element.34, bf16[1024,1024]{1,0:T(8,128)(2,1)S(1)} %copy-done.22), kind=kOutput, calls=%fused_computation.86 | convolution fusion | flops 1073741824 | bytes 5242880 | tf_op jit(solution)/shard_map/dot_general | solution.py:754
  109.9 2.5 %convolution_convert_fusion.4.part_mlp = bf16[512,1024]{1,0:T(8,128)(2,1)} fusion(bf16[1024,1024]{1,0:T(8,128)(2,1)S(1)} %get-tuple-element.33, f32[512,1024]{1,0:T(8,128)S(1)} %fusion.44, f32[1024]{0:T(1024)S(1)} %add.95), kind=kOutput, calls=%fused_computation.36 | convolution fusion | flops 1079508992 | bytes 5246976 | tf_op jit(solution)/shard_map/dot_general | solution.py:757
  112.4 2.5 %convert_reduce_fusion.1 = (f32[1024]{0:T(1024)S(1)}, bf16[512,1024]{1,0:T(8,128)(2,1)S(1)}) fusion(f32[512,1024]{1,0:T(8,128)S(1)} %fusion.44, f32[1024]{0:T(1024)S(1)} %add.95, bf16[512,1024]{1,0:T(8,128)(2,1)S(1)} %copy-done.26, bf16[1024,1024]{1,0:T(8,128)(2,1)S(1)} %get-tuple-element.33), kind=kOutput, calls=%fused_computation.23 | convolution fusion | flops 1085799424 | bytes 6299648 | tf_op jit(solution)/shard_map/dot_general | solution.py:758
  115.1 1.6 convolution_convert_fusion.1.grad_down
  116.8 1.3 convolution_convert_fusion.5.part_norm
  118.1 29.6 %back.1 = (f32[128,1024]{1,0:T(8,128)S(1)}, bf16[512,1024]{1,0:T(8,128)(2,1)S(1)}, f32[8,1024]{1,0:T(8,128)S(1)}, f32[1024,128]{1,0:T(8,128)S(1)}) custom-call(bf16[512,1024]{1,0:T(8,128)(2,1)S(1)} %convolution_convert_fusion.5.part_norm, f32[128,1024]{1,0:T(8,128)S(1)} %get-tuple-element.36.mid, bf16[128,1024]{1,0:T(8,128)(2,1)S(1)} %copy-done.7, ...), custom_call_target="tpu_custom_call" | custom-call | tf_op jit(solution)/shard_map/back/pallas_call | solution.py:771
  147.7 1.2 convolution_convert_fusion.9
  148.9 4.4 %convolution_convert_fusion.8 = bf16[4,64,512]{2,1,0:T(8,128)(2,1)} fusion(bf16[512,4,64]{0,2,1:T(8,128)(2,1)} %bitcast.113, f32[4,512]{1,0:T(4,128)S(1)} %get-tuple-element.95, f32[512,512]{0,1:T(8,128)} %subtract_convert_fusion, f32[4]{0:T(128)S(1)} %multiply_exponential_fusion, pred[512,512]{0,1:T(8,128)(4,1)} %copy-done.38, ...), kind=kOutput, calls=%fused_computation.42 | convolution fusion | flops 275909120 | bytes 2367504 | tf_op jit(solution)/shard_map/hqk,qhd->khd/dot_general | solution.py:807
  153.5 1.3 convolution_convert_fusion.7.grad_out
  154.8 3.0 %convolution_convert_fusion.grad_up = bf16[1024,1024]{1,0:T(8,128)(2,1)S(1)} fusion(bf16[512,1024]{1,0:T(8,128)(2,1)} %get-tuple-element.34, bf16[512,1024]{1,0:T(8,128)(2,1)} %copy-done.40), kind=kOutput, calls=%fused_computation.31 | convolution fusion | flops 1074790400 | bytes 4194304 | tf_op jit(solution)/shard_map/dot_general | solution.py:766
  157.8 0.9 multiply_reduce_fusion
  158.8 1.2 multiply_convert_fusion
  160.0 0.8 fusion.21
  161.5 2.0 convolution_convert_fusion.3.part
  163.7 2.6 %convolution_convert_fusion.2.grad_qkv = bf16[1024,768]{1,0:T(8,128)(2,1)} fusion(bf16[512,256]{0,1:T(8,128)(2,1)S(1)} %bitcast.100, bf16[512,256]{0,1:T(8,128)(2,1)S(1)} %bitcast.87, bf16[512,256]{0,1:T(8,128)(2,1)S(1)} %bitcast.90, bf16[512,1024]{1,0:T(8,128)(2,1)S(1)} %get-tuple-element.28, f32[1024]{0:T(1024)S(1)} %bitcast.110, f32[1024]{0:T(1024)S(1)} %bitcast.108, ...), kind=kOutput, calls=%fused_computation.33 | convolution fusion | flops 811597824 | bytes 3420160 | tf_op jit(solution)/shard_map/dot_general | solution.py:814
  166.7 1.0 copy-done.2
  167.7 1.0 copy-done.3
  168.8 1.4 copy-done.4
  170.2 1.2 copy-done.5
  171.4 1.2 copy-done.6
  172.6 1.0 copy-done.11
  173.7 54.5 %last.1 = (bf16[128,1024]{1,0:T(8,128)(2,1)S(1)}, bf16[128,1024]{1,0:T(8,128)(2,1)S(1)}, f32[8,128]{1,0:T(8,128)S(1)}, f32[256,128]{1,0:T(8,128)S(1)}, f32[128,1024]{1,0:T(8,128)S(1)}, /*index=5*/f32[128,768]{1,0:T(8,128)S(1)}) custom-call(bf16[512,1024]{1,0:T(8,128)(2,1)S(1)} %copy-done.6, bf16[512,1024]{1,0:T(8,128)(2,1)S(1)} %copy-done.5, ...), custom_call_target="tpu_custom_call" | custom-call | tf_op jit(solution)/shard_map/last/pallas_call | solution.py:828
  228.2 0.7 copy-done.12
  228.9 0.7 copy-done.14
  229.6 0.7 copy-done.16
  230.3 0.7 copy-done.18
  231.0 0.7 reshape_squeeze.15
  231.7 0.7 reshape_squeeze.14
  232.4 1.1 copy.73
  233.5 0.9 copy.74
  234.4 1.7 copy.87
  236.1 0.7 copy.88
  237.4 0.7 copy.90
  238.1 0.8 copy.91
  238.9 0.8 copy.92
  (119 shorter events, 5.8 us)
Async XLA Ops:
  0.6 6.1 %copy-start = (bf16[128,1024]{1,0:T(8,128)(2,1)S(1)}, bf16[128,1024]{1,0:T(8,128)(2,1)}, u32[]{:S(2)}) copy-start(bf16[128,1024]{1,0:T(8,128)(2,1)} %tok.5) | copy-start | bytes 786436
  0.7 6.1 %copy-start.7 = (bf16[128,1024]{1,0:T(8,128)(2,1)S(1)}, bf16[128,1024]{1,0:T(8,128)(2,1)}, u32[]{:S(2)}) copy-start(bf16[128,1024]{1,0:T(8,128)(2,1)} %cot.3) | copy-start | bytes 786436
  0.7 6.1 %copy-start.17 = (bf16[128,1024]{1,0:T(8,128)(2,1)S(1)}, bf16[128,1024]{1,0:T(8,128)(2,1)}, u32[]{:S(2)}) copy-start(bf16[128,1024]{1,0:T(8,128)(2,1)} %up.1) | copy-start | bytes 786436
  0.7 6.1 %copy-start.20 = (bf16[256,128]{1,0:T(8,128)(2,1)S(1)}, bf16[256,128]{1,0:T(8,128)(2,1)}, u32[]{:S(2)}) copy-start(bf16[256,128]{1,0:T(8,128)(2,1)} %out.1) | copy-start | bytes 196612
  5.6 61.2 %copy-start.38 = (pred[512,512]{0,1:T(8,128)(4,1)}, pred[512,512]{0,1:T(8,128)(4,1)S(1)}, u32[]{:S(2)}) copy-start(pred[512,512]{0,1:T(8,128)(4,1)S(1)} %fusion.24) | copy-start | bytes 786436
  59.9 1.0 copy-start.25
  60.8 1.3 copy-start.21
  60.8 1.8 copy-start.23
  65.8 6.3 %copy-start.33 = (bf16[512,1,256]{0,2,1:T(8,128)(2,1)}, bf16[512,1,256]{0,2,1:T(8,128)(2,1)S(1)}, u32[]{:S(2)}) copy-start(bf16[512,1,256]{0,2,1:T(8,128)(2,1)S(1)} %slice.93) | copy-start | bytes 786436
  66.8 5.3 %copy-start.28 = (bf16[512,4,64]{0,2,1:T(8,128)(2,1)}, bf16[512,4,64]{0,2,1:T(8,128)(2,1)S(1)}, u32[]{:S(2)}) copy-start(bf16[512,4,64]{0,2,1:T(8,128)(2,1)S(1)} %add_convert_fusion.1) | copy-start | bytes 786436
  66.8 5.3 %copy-start.35 = (f32[512,1,256]{0,2,1:T(8,128)S(1)}, f32[512,1,256]{0,2,1:T(8,128)}, u32[]{:S(2)}) copy-start(f32[512,1,256]{0,2,1:T(8,128)} %get-tuple-element.86) | copy-start | bytes 1572868
  72.1 4.2 %copy-start.13 = (bf16[1024,128]{1,0:T(8,128)(2,1)S(1)}, bf16[1024,128]{1,0:T(8,128)(2,1)}, u32[]{:S(2)}) copy-start(bf16[1024,128]{1,0:T(8,128)(2,1)} %down.1) | copy-start | bytes 786436
  75.8 31.5 %copy-start.31 = (bf16[4,64,512]{2,1,0:T(8,128)(2,1)}, bf16[4,64,512]{2,1,0:T(8,128)(2,1)S(1)}, u32[]{:S(2)}) copy-start(bf16[4,64,512]{2,1,0:T(8,128)(2,1)S(1)} %convolution_convert_fusion.10) | copy-start | bytes 786436
  75.8 31.5 %copy-start.22 = (bf16[1024,1024]{1,0:T(8,128)(2,1)S(1)}, bf16[1024,1024]{1,0:T(8,128)(2,1)}, u32[]{:S(2)}) copy-start(bf16[1024,1024]{1,0:T(8,128)(2,1)} %copy-done.21) | copy-start | bytes 6291460
  107.2 10.8 %copy-start.1 = (f32[128,1024]{1,0:T(8,128)}, f32[128,1024]{1,0:T(8,128)S(1)}, u32[]{:S(2)}) copy-start(f32[128,1024]{1,0:T(8,128)S(1)} %get-tuple-element.36.mid) | copy-start | bytes 1572868
  109.9 2.5 %copy-start.26 = (bf16[512,1024]{1,0:T(8,128)(2,1)S(1)}, bf16[512,1024]{1,0:T(8,128)(2,1)}, u32[]{:S(2)}) copy-start(bf16[512,1024]{1,0:T(8,128)(2,1)} %copy-done.25) | copy-start | bytes 3145732
  114.9 1.8 copy-start.40
  118.1 30.8 %copy-start.29 = (bf16[512,4,64]{0,2,1:T(8,128)(2,1)S(1)}, bf16[512,4,64]{0,2,1:T(8,128)(2,1)}, u32[]{:S(2)}) copy-start(bf16[512,4,64]{0,2,1:T(8,128)(2,1)} %copy-done.28) | copy-start | bytes 786436
  147.7 1.2 copy-start.8
  147.7 1.2 copy-start.10
  148.9 4.6 %copy-start.32 = (bf16[4,64,512]{2,1,0:T(8,128)(2,1)S(1)}, bf16[4,64,512]{2,1,0:T(8,128)(2,1)}, u32[]{:S(2)}) copy-start(bf16[4,64,512]{2,1,0:T(8,128)(2,1)} %copy-done.31) | copy-start | bytes 786436
  154.8 3.0 %copy-start.27 = (f32[4,512,512]{1,2,0:T(8,128)S(1)}, f32[4,512,512]{1,2,0:T(8,128)}, u32[]{:S(2)}) copy-start(f32[4,512,512]{1,2,0:T(8,128)} %get-tuple-element.96) | copy-start | bytes 12582916
  154.8 3.0 %copy-start.36 = (f32[512,1,256]{0,2,1:T(8,128)S(1)}, f32[512,1,256]{0,2,1:T(8,128)}, u32[]{:S(2)}) copy-start(f32[512,1,256]{0,2,1:T(8,128)} %get-tuple-element.86) | copy-start | bytes 1572868
  154.8 3.0 %copy-start.39 = (bf16[512,256]{0,1:T(8,128)(2,1)S(1)}, bf16[512,256]{0,1:T(8,128)(2,1)}, u32[]{:S(2)}) copy-start(bf16[512,256]{0,1:T(8,128)(2,1)} %convolution_convert_fusion.9) | copy-start | bytes 786436
  158.8 1.2 copy-start.30
  160.0 1.0 copy-start.34
  160.0 1.5 copy-start.24
  160.0 1.5 copy-start.37
  166.7 1.0 copy-start.2
  167.7 1.0 copy-start.3
  168.8 1.4 copy-start.4
  170.2 1.2 copy-start.5
  171.4 1.2 copy-start.6
  172.6 1.0 copy-start.11
  228.2 0.7 copy-start.12
  228.9 0.7 copy-start.14
  229.6 0.7 copy-start.16
  230.3 0.7 copy-start.18
  231.0 7.9 %copy-start.9 = (f32[1024,128]{1,0:T(8,128)S(1)}, f32[1024,128]{1,0:T(8,128)}, u32[]{:S(2)}) copy-start(f32[1024,128]{1,0:T(8,128)} %copy-done.8) | copy-start | bytes 1572868
  231.0 5.1 %copy-start.15 = (bf16[128,1024]{1,0:T(8,128)(2,1)S(1)}, bf16[128,1024]{1,0:T(8,128)(2,1)}, u32[]{:S(2)}) copy-start(bf16[128,1024]{1,0:T(8,128)(2,1)} %copy-done.14) | copy-start | bytes 786436
  231.0 6.4 %copy-start.19 = (f32[256,128]{1,0:T(8,128)S(1)}, f32[256,128]{1,0:T(8,128)}, u32[]{:S(2)}) copy-start(f32[256,128]{1,0:T(8,128)} %copy-done.18) | copy-start | bytes 393220

commit v3 on v2

--- a/solution.py
+++ b/solution.py
@@ -352,11 +352,12 @@
 
 
 class DpScatter:
-    def __init__(self, here, part, total, axis, y_buf, z_out, z_in, sems):
+    def __init__(self, here, part, total, axis, y_buf, z_out, z_in, sems, own=None):
+        self.own, self.locals = own, []
         self.here, self.part, self.total, self.axis = here, part, total, axis
         self.y_buf, self.z_out, self.z_in = y_buf, z_out, z_in
         self.send, self.recv = sems
-        self.size = total.shape[axis]
+        self.size = y_buf.shape[1 + axis]
         self.y_flights, self.z_flights = [], []
 
     def slot(self, owner):
@@ -371,12 +372,21 @@
         here = self.here
         src = self.slot(here.owner(here.z_prev(k), here.other_y))
         self.y_flights.append(self.fly(src, self.y_buf.at[k - 1], k - 1, here.y_peer()))
+        if self.own is not None:
+            mine = self.slot(here.owner(here.z_prev(k), here.y))
+            local = pltpu.make_async_copy(mine, self.own[0].at[k - 1], self.own[1].at[k - 1])
+            local.start()
+            self.locals.append(local)
 
     def sum(self, k):
         here = self.here
         self.y_flights[k - 1].wait_recv()
-        own = self.slot(here.owner(here.z_prev(k), here.y))[...].astype(jnp.float32)
-        acc = own + self.y_buf[k - 1].astype(jnp.float32)
+        if self.own is None:
+            own = self.slot(here.owner(here.z_prev(k), here.y))[...]
+        else:
+            self.locals[k - 1].wait()
+            own = self.own[0][k - 1]
+        acc = own.astype(jnp.float32) + self.y_buf[k - 1].astype(jnp.float32)
         if k > 1:
             self.z_flights[k - 2].wait_recv()
             acc = acc + self.z_in[k - 2].astype(jnp.float32)
@@ -389,7 +399,13 @@
         )
 
     def finish(self):
-        self.total[...] = self.sum(Z_COUNT)
+        acc = self.sum(Z_COUNT)
+        if len(self.total.shape) == 3:
+            width = self.total.shape[2]
+            for i in range(self.total.shape[0]):
+                self.total[i] = acc[:, i * width : (i + 1) * width]
+        else:
+            self.total[...] = acc
         for flight in self.y_flights + self.z_flights:
             flight.wait_send()
 
@@ -422,7 +438,8 @@
 
 
 class TensorScatter:
-    def __init__(self, here, part, buf, send, recv):
+    def __init__(self, here, part, buf, send, recv, own=None):
+        self.own = own
         self.here, self.part, self.buf = here, part, buf
         self.send, self.recv = send, recv
         self.rows = buf.shape[1]
@@ -440,11 +457,19 @@
             )
             flight.start()
             self.flights.append(flight)
+        if self.own is not None:
+            mine = block_of(self.part, here.t, self.rows, 0)
+            self.local = pltpu.make_async_copy(mine, self.own[0], self.own[1])
+            self.local.start()
 
     def total(self):
         for flight in self.flights:
             flight.wait_recv()
-        acc = block_of(self.part, self.here.t, self.rows, 0)[...].astype(jnp.float32)
+        if self.own is None:
+            acc = block_of(self.part, self.here.t, self.rows, 0)[...].astype(jnp.float32)
+        else:
+            self.local.wait()
+            acc = self.own[0][...].astype(jnp.float32)
         for k in range(T_COUNT - 1):
             acc = acc + self.buf[k].astype(jnp.float32)
         return acc
@@ -479,7 +504,7 @@
         compiler_params=pltpu.CompilerParams(
             collective_id=collective_id,
             has_side_effects=True,
-            vmem_limit_bytes=44 * 1024 * 1024,
+            vmem_limit_bytes=(56 if collective_id == 4 else 24) * 1024 * 1024,
         ),
     )
 
@@ -607,17 +632,25 @@
 ):
     here = Place()
     here.barrier()
+    owned = scratch[20:26]
+    part_own, mlp_own, mid_own, grad_own, part_sem, mlp_sem, mid_sem, grad_sem = scratch[26:]
     plan = ((grad_out, total_out, 1), (grad_up, total_up, 0), (grad_qkv, total_qkv, 0))
     big = []
     for i, (ref, total, axis) in enumerate(plan):
         group = scratch[5 * i : 5 * i + 5]
-        item = DpScatter(here, ref, total, axis, *group[:3], group[3:])
+        item = DpScatter(
+            here, ref, total, axis, *group[:3], group[3:], owned[2 * i : 2 * i + 2]
+        )
         item.send_y(1)
         big.append(item)
-    scatter = TensorScatter(here, part, buf, t_send, t_recv)
+    scatter = TensorScatter(here, part, buf, t_send, t_recv, (part_own, part_sem))
     scatter.start()
-    second = TensorScatter(here, part_mlp, buf_mlp, m_send, m_recv)
+    second = TensorScatter(here, part_mlp, buf_mlp, m_send, m_recv, (mlp_own, mlp_sem))
     second.start()
+    mid_copy = pltpu.make_async_copy(mid, mid_own, mid_sem)
+    mid_copy.start()
+    grad_copy = pltpu.make_async_copy(grad_mid, grad_own, grad_sem)
+    grad_copy.start()
     for item in big:
         item.send_y(2)
     for item in big:
@@ -626,7 +659,8 @@
     inner, gain_grad, shift_grad = norm_back(
         scatter.total(), tok[...].astype(jnp.float32), vec[0:1]
     )
-    grad_tok[...] = (grad_mid[...] + inner).astype(jnp.bfloat16)
+    grad_copy.wait()
+    grad_tok[...] = (grad_own[...] + inner).astype(jnp.bfloat16)
     width = total_small.shape[1]
     for d in range(Z_COUNT * Y_COUNT):
         cols = slice(d * width, (d + 1) * width)
@@ -641,7 +675,8 @@
         item.step(2)
         item.send_y(4)
     small.step(1)
-    result[...] = (mid[...] + second.total() + vec[5:6]).astype(jnp.bfloat16)
+    mid_copy.wait()
+    result[...] = (mid_own[...] + second.total() + vec[5:6]).astype(jnp.bfloat16)
     small.step(2)
     for item in big:
         item.step(3)
@@ -834,9 +869,9 @@
             shape((8, cols), f32),
             shape((local_width, cols), f32),
             shape((width // dp, hidden), f32),
-            shape((width // dp, qkv_wide), f32),
+            shape((3, width // dp, local_width), f32),
         ],
-        [IN_VMEM] * 11,
+        [ANYWHERE] * 2 + [IN_VMEM] + [ANYWHERE] * 2 + [IN_VMEM] * 3 + [ANYWHERE] * 3,
         [IN_VMEM] * 6,
         [
             pltpu.VMEM((3, rows, width), bf16),
@@ -850,14 +885,20 @@
         + scatter_scratch((local_width, cols), bf16)
         + scatter_scratch((width // dp, hidden), bf16)
         + scatter_scratch((width // dp, qkv_wide), bf16)
-        + scatter_scratch((8, cols), f32),
+        + scatter_scratch((8, cols), f32)
+        + [pltpu.VMEM((4, local_width, cols), bf16), DMA((4,))]
+        + [pltpu.VMEM((4, width // dp, hidden), bf16), DMA((4,))]
+        + [pltpu.VMEM((4, width // dp, qkv_wide), bf16), DMA((4,))]
+        + [pltpu.VMEM((rows, width), bf16)] * 2
+        + [pltpu.VMEM((rows, width), f32)] * 2
+        + [DMA] * 4,
         4,
     )(part_first, part_mlp, tokens, middle, grad_middle, vec_full, sums, bias_rows, grad_out, grad_up, grad_qkv)
     return (
         output,
         grad_tokens,
         total_small[:6],
-        total_qkv.reshape(w_qkv.shape),
+        total_qkv.transpose(1, 0, 2),
         total_small[6, : qv_bias.size].reshape(qv_bias.shape),
         total_out,
         total_up,

time: 240 us -> 236 us (0.983)
  local copies, waits for them, and re-layouts: 24.2 us -> 19.3 us
    unnamed x90 -> x70, local copies, waits for them, and re-layouts: 19.5 us -> 14.3 us
    pallas_call x1, Pallas kernels: 54.5 us -> 57 us  [on_device_direct(): call(last_kernel, 'last', [shape((rows, width), bf16), shape((rows, width...]
where the time goes in v3:
time: 236 us; the launch traced here: 235 us
  Pallas kernels  170 us (72%)
  matrix products  38 us (16%)
  local copies, waits for them, and re-layouts  19.3 us (8%)
  other arithmetic  7.31 us (3%)
    pallas_call x1, Pallas kernels, on_device_direct(): call(last_kernel, 'last', [shape((rows, width), bf16), shape((rows, width...  57 us
    pallas_call x1, Pallas kernels, on_device_direct(): call(gather_kernel, 'gather_inputs', [shape((group_size, width), bf16), s...  53 us
    pallas_call x1, Pallas kernels, on_device_direct(): call(middle_kernel, 'middle', [shape((rows, width), f32), shape((group_si...  30 us
    pallas_call x1, Pallas kernels, on_device_direct(): call(back_kernel, 'back', [shape((rows, width), f32), shape((group_size,...  29.6 us
    unnamed x70, local copies, waits for them, and re-layouts  14.3 us
    sub x1, matrix products, on_device_direct(): exponent = jnp.exp(scores - row_max)  5.15 us

profile of v3, /device:TPU:0, one launch (start us, length us, event | category | flops | bytes accessed | tf_op | source)
XLA Modules:
  0.0 235.4 jit_solution(432421591751678202)
XLA Ops:
  0.7 0.9 reduce-window.8
  1.7 0.7 convert.21
  2.5 0.7 convert.19
  3.2 0.7 convert.20
  4.1 1.1 copy.53
  5.6 1.2 subtract_convert_fusion
  6.7 53.0 %gather_inputs.1 = (bf16[512,1024]{1,0:T(8,128)(2,1)S(1)}, bf16[512,1024]{1,0:T(8,128)(2,1)S(1)}, bf16[128,128]{1,0:T(8,128)(2,1)S(1)}, bf16[1024,768]{1,0:T(8,1...) custom-call(bf16[128,1024]{1,0:T(8,128)(2,1)S(1)} %copy-done, ...), custom_call_target="tpu_custom_call" | custom-call | tf_op jit(solution)/shard_map/gather_inputs/pallas_call | solution.py:725
  59.8 1.3 copy-done.13
  61.1 1.0 copy-done.17
  62.1 0.2 convert_reduce_fusion
  62.3 0.4 fusion.4
  62.8 0.5 copy-done.15
  63.8 2.6 %fusion.36 = f32[512,768]{0,1:T(8,128)S(1)} fusion(bf16[1024,768]{1,0:T(8,128)(2,1)} %copy-done.15, bf16[512,1024]{1,0:T(8,128)(2,1)S(1)} %get-tuple-element.28, f32[1024]{0:T(1024)S(1)} %bitcast.109, f32[1024]{0:T(1024)S(1)} %bitcast.107, f32[512]{0:T(512)S(1)} %add_rsqrt_fusion, f32[512]{0:T(512)S(1)} %broadcast_multiply_fusion), kind=kOutput, calls=%fused_computation.80 | convolution fusion | flops 808452096 | bytes 4206592 | tf_op jit(solution)/shard_map/dot_general | solution.py:754
  66.4 0.9 fusion.39
  67.4 5.1 %fusion.43 = (f32[4,512]{1,0:T(4,128)S(1)}, f32[4,512,512]{1,2,0:T(8,128)}) fusion(f32[512,512]{0,1:T(8,128)} %subtract_convert_fusion, f32[4]{0:T(128)S(1)} %multiply_exponential_fusion, pred[512,512]{0,1:T(8,128)(4,1)S(1)} %fusion.24, bf16[512,4,64]{0,2,1:T(8,128)(2,1)S(1)} %add_convert_fusion.1, bf16[512,4,64]{0,2,1:T(8,128)(2,1)S(1)} %bitcast.89), kind=kOutput, calls=%fused_computation.85 | convolution fusion | flops 140509696 | bytes 6037520 | tf_op jit(solution)/shard_map/sub | solution.py:762
  72.6 3.7 %convolution_convert_fusion.10 = bf16[4,64,512]{2,1,0:T(8,128)(2,1)S(1)} fusion(f32[512,4,64]{0,2,1:T(8,128)} %bitcast.94, f32[4,64]{1,0:T(4,128)S(1)} %add.92, f32[4,512]{1,0:T(4,128)S(1)} %get-tuple-element.59, f32[512,512]{0,1:T(8,128)} %subtract_convert_fusion, f32[4]{0:T(128)S(1)} %multiply_exponential_fusion, pred[512,512]{0,1:T(8,128)(4,1)S(1)} %fusion.24, ...), kind=kOutput, calls=%fused_computation.44 | convolution fusion | flops 276171264 | bytes 2630672 | tf_op jit(solution)/shard_map/hqk,khd->qhd/dot_general | solution.py:767
  76.3 0.5 convolution_convert_fusion.6.part
  76.8 30.0 %middle.1 = (f32[128,1024]{1,0:T(8,128)S(1)}, bf16[512,1024]{1,0:T(8,128)(2,1)S(1)}, bf16[1024,1024]{1,0:T(8,128)(2,1)S(1)}) custom-call(bf16[512,1024]{1,0:T(8,128)(2,1)S(1)} %convolution_convert_fusion.6.part, bf16[128,1024]{1,0:T(8,128)(2,1)S(1)} %copy-done, f32[8,1024]{1,0:T(8,128)S(1)} %get-tuple-element.51.vec, bf16[1024,128]{1,0:T(8,128)(2,1)S(1)} %copy-done.9), custom_call_target="tpu_custom_call" | custom-call | tf_op jit(solution)/shard_map/middle/pallas_call | solution.py:773
  106.8 1.2 fusion.44
  108.1 2.6 %convolution_convert_fusion.4.part_mlp = bf16[512,1024]{1,0:T(8,128)(2,1)} fusion(bf16[1024,1024]{1,0:T(8,128)(2,1)S(1)} %get-tuple-element.33, f32[512,1024]{1,0:T(8,128)S(1)} %fusion.44, f32[1024]{0:T(1024)S(1)} %add.95), kind=kOutput, calls=%fused_computation.36 | convolution fusion | flops 1079508992 | bytes 5246976 | tf_op jit(solution)/shard_map/dot_general | solution.py:792
  110.7 2.7 %convert_reduce_fusion.1 = (f32[1024]{0:T(1024)S(1)}, bf16[512,1024]{1,0:T(8,128)(2,1)S(1)}) fusion(f32[512,1024]{1,0:T(8,128)S(1)} %fusion.44, f32[1024]{0:T(1024)S(1)} %add.95, bf16[512,1024]{1,0:T(8,128)(2,1)S(1)} %copy-done.18, bf16[1024,1024]{1,0:T(8,128)(2,1)S(1)} %get-tuple-element.33), kind=kOutput, calls=%fused_computation.23 | convolution fusion | flops 1085799424 | bytes 6299648 | tf_op jit(solution)/shard_map/dot_general | solution.py:793
  113.5 1.6 convolution_convert_fusion.1.grad_down
  115.1 1.3 convolution_convert_fusion.5.part_norm
  116.4 29.6 %back.1 = (f32[128,1024]{1,0:T(8,128)S(1)}, bf16[512,1024]{1,0:T(8,128)(2,1)S(1)}, f32[8,1024]{1,0:T(8,128)S(1)}, f32[1024,128]{1,0:T(8,128)S(1)}) custom-call(bf16[512,1024]{1,0:T(8,128)(2,1)S(1)} %convolution_convert_fusion.5.part_norm, f32[128,1024]{1,0:T(8,128)S(1)} %get-tuple-element.36.mid, bf16[128,1024]{1,0:T(8,128)(2,1)S(1)} %copy-done.2, ...), custom_call_target="tpu_custom_call" | custom-call | tf_op jit(solution)/shard_map/back/pallas_call | solution.py:806
  146.1 0.5 convolution_convert_fusion.9
  146.6 0.3 copy-done.6
  147.1 3.7 %convolution_convert_fusion.8 = bf16[4,64,512]{2,1,0:T(8,128)(2,1)S(1)} fusion(bf16[512,4,64]{0,2,1:T(8,128)(2,1)S(1)} %bitcast.113, f32[4,512]{1,0:T(4,128)S(1)} %get-tuple-element.59, f32[512,512]{0,1:T(8,128)} %subtract_convert_fusion, f32[4]{0:T(128)S(1)} %multiply_exponential_fusion, pred[512,512]{0,1:T(8,128)(4,1)} %copy-done.27, ...), kind=kOutput, calls=%fused_computation.42 | convolution fusion | flops 275909120 | bytes 2367504 | tf_op jit(solution)/shard_map/hqk,qhd->khd/dot_general | solution.py:842
  151.0 1.2 convolution_convert_fusion.7.grad_out
  152.2 4.3 %convolution_convert_fusion.grad_up = bf16[1024,1024]{1,0:T(8,128)(2,1)} fusion(bf16[512,1024]{1,0:T(8,128)(2,1)} %copy-done.19, bf16[512,1024]{1,0:T(8,128)(2,1)} %copy-done.30), kind=kOutput, calls=%fused_computation.31 | convolution fusion | flops 1074790400 | bytes 4194304 | tf_op jit(solution)/shard_map/dot_general | solution.py:801
  156.5 1.0 multiply_reduce_fusion
  157.5 1.2 multiply_convert_fusion
  158.7 0.8 fusion.21
  159.6 0.5 fusion.20
  160.2 2.0 convolution_convert_fusion.3.part
  162.4 2.6 %convolution_convert_fusion.2.grad_qkv = bf16[1024,768]{1,0:T(8,128)(2,1)} fusion(bf16[512,256]{0,1:T(8,128)(2,1)S(1)} %bitcast.99, bf16[512,256]{0,1:T(8,128)(2,1)S(1)} %bitcast.85, bf16[512,256]{0,1:T(8,128)(2,1)S(1)} %bitcast.88, bf16[512,1024]{1,0:T(8,128)(2,1)S(1)} %get-tuple-element.28, f32[1024]{0:T(1024)S(1)} %bitcast.110, f32[1024]{0:T(1024)S(1)} %bitcast.108, ...), kind=kOutput, calls=%fused_computation.33 | convolution fusion | flops 811597824 | bytes 3420160 | tf_op jit(solution)/shard_map/dot_general | solution.py:849
  165.3 0.7 maximum_bitcast_fusion.1.bias_rows
  166.0 57.0 %last.1 = (bf16[128,1024]{1,0:T(8,128)(2,1)}, bf16[128,1024]{1,0:T(8,128)(2,1)}, f32[8,128]{1,0:T(8,128)}, f32[256,128]{1,0:T(8,128)}, f32[128,1024]{1,0:T(8,128)}, /*index=5*/f32[3,128,256]{2,1,0:T(8,128)}) custom-call(bf16[512,1024]{1,0:T(8,128)(2,1)} %convolution_convert_fusion.3.part, bf16[512,1024]{1,0:T(8,128)(2,1)} %convolution_convert_fusion.4.part_mlp, ...), custom_call_target="tpu_custom_call" | custom-call | tf_op jit(solution)/shard_map/last/pallas_call | solution.py:863
  223.1 0.8 slice_reduce_fusion.1
  223.9 0.7 slice_reduce_fusion.2
  224.6 0.7 reshape_squeeze.15
  225.2 0.7 reshape_squeeze.14
  225.9 1.7 copy.81
  227.6 1.7 copy.82
  229.2 1.3 copy.83
  230.5 1.8 copy.84
  232.3 1.6 copy.85
  233.8 0.8 copy.86
  234.6 0.8 copy.87
  (98 shorter events, 2.6 us)
Async XLA Ops:
  0.6 6.1 %copy-start = (bf16[128,1024]{1,0:T(8,128)(2,1)S(1)}, bf16[128,1024]{1,0:T(8,128)(2,1)}, u32[]{:S(2)}) copy-start(bf16[128,1024]{1,0:T(8,128)(2,1)} %tok.5) | copy-start | bytes 786436
  0.7 6.1 %copy-start.2 = (bf16[128,1024]{1,0:T(8,128)(2,1)S(1)}, bf16[128,1024]{1,0:T(8,128)(2,1)}, u32[]{:S(2)}) copy-start(bf16[128,1024]{1,0:T(8,128)(2,1)} %cot.3) | copy-start | bytes 786436
  0.7 6.1 %copy-start.10 = (bf16[128,1024]{1,0:T(8,128)(2,1)S(1)}, bf16[128,1024]{1,0:T(8,128)(2,1)}, u32[]{:S(2)}) copy-start(bf16[128,1024]{1,0:T(8,128)(2,1)} %up.1) | copy-start | bytes 786436
  0.7 6.1 %copy-start.11 = (bf16[256,128]{1,0:T(8,128)(2,1)S(1)}, bf16[256,128]{1,0:T(8,128)(2,1)}, u32[]{:S(2)}) copy-start(bf16[256,128]{1,0:T(8,128)(2,1)} %out.1) | copy-start | bytes 196612
  5.5 67.0 %copy-start.27 = (pred[512,512]{0,1:T(8,128)(4,1)}, pred[512,512]{0,1:T(8,128)(4,1)S(1)}, u32[]{:S(2)}) copy-start(pred[512,512]{0,1:T(8,128)(4,1)S(1)} %fusion.24) | copy-start | bytes 786436
  59.8 1.3 copy-start.13
  61.1 1.0 copy-start.17
  62.1 1.2 copy-start.15
  62.1 14.2 %copy-start.4 = (bf16[256,1024]{1,0:T(8,128)(2,1)}, bf16[256,1024]{1,0:T(8,128)(2,1)S(1)}, u32[]{:S(2)}) copy-start(bf16[256,1024]{1,0:T(8,128)(2,1)S(1)} %get-tuple-element.32) | copy-start | bytes 1572868
  63.3 53.1 %copy-start.3 = (f32[8,1024]{1,0:T(8,128)}, f32[8,1024]{1,0:T(8,128)S(1)}, u32[]{:S(2)}) copy-start(f32[8,1024]{1,0:T(8,128)S(1)} %get-tuple-element.51.vec) | copy-start | bytes 98308
  66.4 6.1 %copy-start.23 = (bf16[512,1,256]{0,2,1:T(8,128)(2,1)}, bf16[512,1,256]{0,2,1:T(8,128)(2,1)S(1)}, u32[]{:S(2)}) copy-start(bf16[512,1,256]{0,2,1:T(8,128)(2,1)S(1)} %slice.93) | copy-start | bytes 786436
  72.6 4.2 %copy-start.9 = (bf16[1024,128]{1,0:T(8,128)(2,1)S(1)}, bf16[1024,128]{1,0:T(8,128)(2,1)}, u32[]{:S(2)}) copy-start(bf16[1024,128]{1,0:T(8,128)(2,1)} %down.1) | copy-start | bytes 786436
  76.3 31.8 %copy-start.21 = (bf16[4,64,512]{2,1,0:T(8,128)(2,1)}, bf16[4,64,512]{2,1,0:T(8,128)(2,1)S(1)}, u32[]{:S(2)}) copy-start(bf16[4,64,512]{2,1,0:T(8,128)(2,1)S(1)} %convolution_convert_fusion.10) | copy-start | bytes 786436
  76.3 30.5 %copy-start.14 = (bf16[1024,1024]{1,0:T(8,128)(2,1)S(1)}, bf16[1024,1024]{1,0:T(8,128)(2,1)}, u32[]{:S(2)}) copy-start(bf16[1024,1024]{1,0:T(8,128)(2,1)} %copy-done.13) | copy-start | bytes 6291460
  106.8 1.3 copy-start.19
  106.8 9.6 %copy-start.1 = (f32[128,1024]{1,0:T(8,128)}, f32[128,1024]{1,0:T(8,128)S(1)}, u32[]{:S(2)}) copy-start(f32[128,1024]{1,0:T(8,128)S(1)} %get-tuple-element.36.mid) | copy-start | bytes 1572868
  108.1 2.6 %copy-start.18 = (bf16[512,1024]{1,0:T(8,128)(2,1)S(1)}, bf16[512,1024]{1,0:T(8,128)(2,1)}, u32[]{:S(2)}) copy-start(bf16[512,1024]{1,0:T(8,128)(2,1)} %copy-done.17) | copy-start | bytes 3145732
  113.4 1.7 copy-start.30
  116.4 29.7 %copy-start.5 = (bf16[256,1024]{1,0:T(8,128)(2,1)S(1)}, bf16[256,1024]{1,0:T(8,128)(2,1)}, u32[]{:S(2)}) copy-start(bf16[256,1024]{1,0:T(8,128)(2,1)} %copy-done.4) | copy-start | bytes 1572868
  146.0 0.8 copy-start.6
  146.1 1.0 copy-start.8
  146.1 4.7 %copy-start.12 = (f32[8,1024]{1,0:T(8,128)}, f32[8,1024]{1,0:T(8,128)S(1)}, u32[]{:S(2)}) copy-start(f32[8,1024]{1,0:T(8,128)S(1)} %get-tuple-element.39.sums) | copy-start | bytes 98308
  147.1 3.7 %copy-start.28 = (bf16[512,256]{0,1:T(8,128)(2,1)}, bf16[512,256]{0,1:T(8,128)(2,1)S(1)}, u32[]{:S(2)}) copy-start(bf16[512,256]{0,1:T(8,128)(2,1)S(1)} %convolution_convert_fusion.9) | copy-start | bytes 786436
  147.1 3.9 %copy-start.22 = (bf16[4,64,512]{2,1,0:T(8,128)(2,1)S(1)}, bf16[4,64,512]{2,1,0:T(8,128)(2,1)}, u32[]{:S(2)}) copy-start(bf16[4,64,512]{2,1,0:T(8,128)(2,1)} %copy-done.21) | copy-start | bytes 786436
  152.2 4.3 %copy-start.20 = (f32[4,512,512]{1,2,0:T(8,128)S(1)}, f32[4,512,512]{1,2,0:T(8,128)}, u32[]{:S(2)}) copy-start(f32[4,512,512]{1,2,0:T(8,128)} %get-tuple-element.60) | copy-start | bytes 12582916
  152.2 4.3 %copy-start.26 = (f32[512,1,256]{0,2,1:T(8,128)S(1)}, f32[512,1,256]{0,2,1:T(8,128)}, u32[]{:S(2)}) copy-start(f32[512,1,256]{0,2,1:T(8,128)} %get-tuple-element.50) | copy-start | bytes 1572868
  152.2 4.3 %copy-start.29 = (bf16[512,256]{0,1:T(8,128)(2,1)S(1)}, bf16[512,256]{0,1:T(8,128)(2,1)}, u32[]{:S(2)}) copy-start(bf16[512,256]{0,1:T(8,128)(2,1)} %copy-done.28) | copy-start | bytes 786436
  158.7 1.0 copy-start.24
  158.7 1.5 copy-start.16
  223.1 10.8 %copy-start.25 = (f32[128,1024]{1,0:T(8,128)S(1)}, f32[128,1024]{1,0:T(8,128)}, u32[]{:S(2)}) copy-start(f32[128,1024]{1,0:T(8,128)} %get-tuple-element.78) | copy-start | bytes 1572868
  223.1 11.6 %copy-start.7 = (f32[1024,128]{1,0:T(8,128)S(1)}, f32[1024,128]{1,0:T(8,128)}, u32[]{:S(2)}) copy-start(f32[1024,128]{1,0:T(8,128)} %copy-done.6) | copy-start | bytes 1572868
